TPU v7x, 32 devices: a whole 2x2x4 slice. The times are simulated.
32 devices in a mesh: nodes: 8 (over z, x), mp: 4 (over y, core).
Axes of the slice: x: 2, y: 2, z: 4, core: 2. Of those that a mesh axis runs over, the one named last changes fastest.
Arguments:
- tokens: bfloat16 [256, 64, 768], P('nodes'), may hold values from -32 to 32
- w_query: bfloat16 [768, 768], P('mp'), may hold values from -0.5 to 0.5
- w_key: bfloat16 [768, 768], P('mp'), may hold values from -0.5 to 0.5
- w_value: bfloat16 [768, 768], P('mp'), may hold values from -0.21875 to 0.21875
- grad_out: bfloat16 [256, 12, 4096], P('nodes', 'mp'), may hold values from -6 to 6
- owned_cls: bfloat16 [768, 16384], P('mp', 'nodes'), may hold values from -24 to 24
- send_rows: int32 [8, 8, 256], P('nodes'), may hold values from 0 to 2047
- neigh_slot: int32 [256, 2, 32], P('nodes'), may hold values from 0 to 2047
- neigh_count: int32 [256, 2], P('nodes'), may hold values from 1 to 32
Outputs:
- context: bfloat16 [256, 12, 4096], P('nodes', 'mp')
- grad_query: float32 [768, 768], P('mp')
- grad_key: float32 [768, 768], P('mp')
- grad_value: float32 [768, 768], P('mp')
- grad_cls: float32 [768, 16384], P('mp', 'nodes')
Inputs may be any that keep to these rules, and one draw needn't show every extreme that they name: send_rows[o, r, :] are rows of owner o's own block; rows may repeat. `neigh_slot`: entries with k >= neigh_count[c, t] are not used.
All inputs are finite; a program needn't handle non-finite values.
Results may differ from a plain program's by a relative error of at most 0.012.
The roundings to bfloat16 on the way count: a program that leaves them out, or rounds other values in their place, can miss the bound.
Values may be sent and summed in bfloat16 or wider, within the bound.
A program may use at most 128 MiB of HBM per device.

v0:
```python
import math

import jax
import jax.numpy as jnp
from jax import lax
from jax.sharding import PartitionSpec as P

HD = 64


def widen_columns(features):
    return lax.all_gather(features, "mp", axis=0, tiled=True)


def local_attend(tokens, virtual, w_query, w_key, w_value, grad_out):
    centres, length, model_width = tokens.shape
    local_width = w_query.shape[0]
    head_count = local_width // HD
    type_count = virtual.shape[1]
    span = type_count + length
    key_input = jnp.concatenate([virtual, tokens], axis=1)
    flat_tokens = tokens.reshape(-1, model_width)
    flat_keys = key_input.reshape(-1, model_width)
    queries = (
        jnp.einsum("nd,od->no", flat_tokens, w_query, preferred_element_type=jnp.float32)
        .astype(jnp.bfloat16)
        .reshape(centres, length, head_count, HD)
    )
    keys = (
        jnp.einsum("nd,od->no", flat_keys, w_key, preferred_element_type=jnp.float32)
        .astype(jnp.bfloat16)
        .reshape(centres, span, head_count, HD)
    )
    values = (
        jnp.einsum("nd,od->no", flat_keys, w_value, preferred_element_type=jnp.float32)
        .astype(jnp.bfloat16)
        .reshape(centres, span, head_count, HD)
    )
    score_scale = 1.0 / math.sqrt(HD)
    scores = (
        jnp.einsum("clhe,cmhe->chlm", queries, keys, preferred_element_type=jnp.float32)
        * score_scale
    )
    attn_probs = jax.nn.softmax(scores, axis=-1)
    probs_low = attn_probs.astype(jnp.bfloat16)
    context = jnp.einsum(
        "chlm,cmhe->chle", probs_low, values, preferred_element_type=jnp.float32
    ).astype(jnp.bfloat16)
    grad_heads = grad_out.reshape(centres, head_count, length, HD)
    prob_grads = jnp.einsum(
        "chle,cmhe->chlm", grad_heads, values, preferred_element_type=jnp.float32
    )
    value_grads = jnp.einsum(
        "chlm,chle->cmhe", probs_low, grad_heads, preferred_element_type=jnp.float32
    ).astype(jnp.bfloat16)
    score_grads = (
        attn_probs
        * (prob_grads - jnp.sum(prob_grads * attn_probs, axis=-1, keepdims=True))
        * score_scale
    )
    score_low = score_grads.astype(jnp.bfloat16)
    query_grads = jnp.einsum(
        "chlm,cmhe->clhe", score_low, keys, preferred_element_type=jnp.float32
    ).astype(jnp.bfloat16)
    key_grads = jnp.einsum(
        "chlm,clhe->cmhe", score_low, queries, preferred_element_type=jnp.float32
    ).astype(jnp.bfloat16)
    part_query = jnp.einsum(
        "no,nd->od",
        query_grads.reshape(-1, local_width),
        flat_tokens,
        preferred_element_type=jnp.float32,
    )
    part_key = jnp.einsum(
        "no,nd->od",
        key_grads.reshape(-1, local_width),
        flat_keys,
        preferred_element_type=jnp.float32,
    )
    part_value = jnp.einsum(
        "no,nd->od",
        value_grads.reshape(-1, local_width),
        flat_keys,
        preferred_element_type=jnp.float32,
    )
    virtual_key = key_grads[:, :type_count].reshape(-1, local_width)
    virtual_value = value_grads[:, :type_count].reshape(-1, local_width)
    virtual_grads = jnp.einsum(
        "no,od->dn", virtual_key, w_key, preferred_element_type=jnp.float32
    ) + jnp.einsum("no,od->dn", virtual_value, w_value, preferred_element_type=jnp.float32)
    return (
        context.reshape(centres, head_count, length * HD),
        part_query,
        part_key,
        part_value,
        virtual_grads,
    )


def body(tokens, w_query, w_key, w_value, grad_out, owned_cls, send_rows, neigh_slot, neigh_count):
    centres = tokens.shape[0]
    model_width = tokens.shape[2]
    local_width = owned_cls.shape[0]
    own_rows = owned_cls.shape[1]
    type_count = neigh_slot.shape[1]
    slot_width = neigh_slot.shape[2]
    send_flat = send_rows[0].reshape(-1)
    outgoing = jnp.take(owned_cls, send_flat, axis=1)
    fetched = lax.all_to_all(outgoing, "nodes", split_axis=1, concat_axis=1, tiled=True)
    slots_total = fetched.shape[1]
    pairs = centres * type_count
    counts = neigh_count.reshape(-1).astype(jnp.float32)
    live_mask = lax.broadcasted_iota(jnp.int32, neigh_slot.shape, 2) < neigh_count[:, :, None]
    live_float = live_mask.astype(jnp.float32).reshape(-1)
    pair_index = lax.broadcasted_iota(jnp.int32, (pairs, slot_width), 0).reshape(-1)
    mixing = (
        jnp.zeros((pairs, slots_total), jnp.float32)
        .at[pair_index, neigh_slot.reshape(-1)]
        .add(live_float)
    )
    mixing_low = mixing.astype(jnp.bfloat16)
    summed = jnp.einsum("dr,nr->dn", fetched, mixing_low, preferred_element_type=jnp.float32)
    part_means = (summed / counts[None, :]).astype(jnp.bfloat16)
    virtual_cols = widen_columns(part_means)
    virtual = virtual_cols.T.reshape(centres, type_count, model_width)
    context, part_query, part_key, part_value, virtual_grads = local_attend(
        tokens, virtual, w_query, w_key, w_value, grad_out
    )
    summed_weights = lax.psum((part_query, part_key, part_value), "nodes")
    shared_grad = (
        lax.psum_scatter(
            virtual_grads.astype(jnp.bfloat16), "mp", scatter_dimension=0, tiled=True
        ).astype(jnp.float32)
        / counts[None, :]
    )
    slot_grads = jnp.dot(
        shared_grad, mixing, precision=lax.Precision.HIGHEST, preferred_element_type=jnp.float32
    )
    returned = lax.all_to_all(
        slot_grads.astype(jnp.bfloat16), "nodes", split_axis=1, concat_axis=1, tiled=True
    ).astype(slot_grads.dtype)
    grad_cls = jnp.zeros((local_width, own_rows), jnp.float32).at[:, send_flat].add(returned)
    return (context, summed_weights[0], summed_weights[1], summed_weights[2], grad_cls)


def solution(mesh):
    in_specs = (
        P("nodes", None, None),
        P("mp", None),
        P("mp", None),
        P("mp", None),
        P("nodes", "mp", None),
        P("mp", "nodes"),
        P("nodes", None, None),
        P("nodes", None, None),
        P("nodes", None),
    )
    out_specs = (
        P("nodes", "mp", None),
        P("mp", None),
        P("mp", None),
        P("mp", None),
        P("mp", "nodes"),
    )
    return jax.shard_map(body, mesh=mesh, in_specs=in_specs, out_specs=out_specs, check_vma=False)
```

profile of v0, /device:TPU:0, one launch (start us, length us, event | category | flops | bytes accessed | tf_op | source)
XLA Modules:
  0.0 353.5 jit_solution(10292123969207134384)
XLA Ops:
  10.9 9.1 %gather_fusion = bf16[2048,192]{1,0:T(8,128)(2,1)} fusion(bf16[192,2048]{0,1:T(8,128)(2,1)S(1)} %copy.69, s32[2048]{0:T(1024)S(1)} %broadcast_clamp_fusion), kind=kCustom, calls=%fused_computation | custom fusion | bytes 1581056 | tf_op jit(solution)/shard_map/jit(_take)/gather | solution.py:108
  24.5 7.3 %all-to-all-start = ((bf16[192,8,256]{2,0,1:T(8,128)(2,1)}), bf16[192,8,256]{2,0,1:T(8,128)(2,1)}, u32[]{:S(2)}, u32[]{:S(2)}) async-start(bf16[192,8,256]{2,0,1:T(8,128)(2,1)} %broadcast_select_fusion), calls=%async_computation | async-start | bytes 1572864 | tf_op jit(solution)/shard_map/all_to_all | solution.py:109
  32.5 12.1 %scatter_custom_fusion.1 = f32[131072]{0:T(1024)} fusion(s32[2048]{0:T(1024)S(1)} %broadcast_select_fusion.1, f32[2048]{0:T(1024)S(1)} %reshape.213, f32[]{:T(128)} %constant.12.clone.1), kind=kCustom, calls=%fused_computation.51 | custom fusion | flops 2048 | bytes 524292
  46.8 3.0 convolution_convert_fusion.2
  49.8 3.4 reshape.175
  53.2 3.4 reshape.183
  59.3 5.6 %all-gather = bf16[4,192,64]{1,2,0:T(8,128)(2,1)S(1)} all-gather(bf16[1,192,64]{1,2,0:T(8,128)(2,1)S(1)} %fusion.26), channel_id=1, replica_groups=mesh['nodes'=8,'mp'=4] {'mp'}, dimensions={0}, use_global_device_ids=true | all-gather | bytes 122880 | tf_op jit(solution)/shard_map/all_gather | solution.py:12
  67.4 4.6 %pad_maximum_fusion = bf16[32,66,768]{2,1,0:T(8,128)(2,1)} fusion(bf16[32,64,768]{2,1,0:T(8,128)(2,1)S(1)} %copy-done.1, bf16[32,2,768]{2,1,0:T(2,128)(2,1)} %reshape.178), kind=kLoop, calls=%fused_computation.7 | loop fusion | flops 6488064 | bytes 6488064 | tf_op jit(solution)/shard_map/concatenate | solution.py:21
  72.0 3.1 reshape.179
  75.1 3.1 convolution_convert_fusion
  78.2 6.8 %reshape.181 = bf16[32,66,3,64]{1,0,3,2:T(8,128)(2,1)} reshape(bf16[2112,192]{0,1:T(8,128)(2,1)} %convolution_convert_fusion) | data formatting | bytes 1622016 | tf_op jit(solution)/shard_map/reshape | solution.py:37
  87.2 6.8 %reshape.180 = bf16[32,66,3,64]{1,0,3,2:T(8,128)(2,1)} reshape(bf16[2112,192]{0,1:T(8,128)(2,1)} %convolution_convert_fusion.1) | data formatting | bytes 1622016 | tf_op jit(solution)/shard_map/reshape | solution.py:32
  93.9 3.4 fusion.13
  97.4 3.2 fusion.50
  104.2 39.9 %fusion.9 = bf16[32,64,3,64]{1,3,2,0:T(8,128)(2,1)} fusion(f32[32,3,66,64]{2,3,1,0:T(8,128)} %fusion.17, bf16[32,66,3,64]{1,0,3,2:T(8,128)(2,1)} %reshape.180, f32[32,3,64,66]{3,2,1,0:T(8,128)} %get-tuple-element.29, f32[32,3,64]{2,1,0:T(4,128)} %get-tuple-element.28), kind=kOutput, calls=%fused_computation.25 | convolution fusion | flops 55142464 | bytes 4866048 | tf_op jit(solution)/shard_map/chlm,cmhe->clhe/dot_general | solution.py:62
  144.2 39.9 %fusion.10 = bf16[32,66,3,64]{1,3,2,0:T(8,128)(2,1)} fusion(f32[32,3,66,64]{2,3,1,0:T(8,128)} %fusion.17, bf16[32,64,3,64]{1,0,3,2:T(8,128)(2,1)} %reshape.175, f32[32,3,64,66]{3,2,1,0:T(8,128)} %get-tuple-element.29, f32[32,3,64]{2,1,0:T(4,128)} %get-tuple-element.28), kind=kOutput, calls=%fused_computation.26 | convolution fusion | flops 55154752 | bytes 4866048 | tf_op jit(solution)/shard_map/chlm,clhe->cmhe/dot_general | solution.py:65
  184.0 15.9 %fusion.11 = bf16[32,66,3,64]{1,3,2,0:T(8,128)(2,1)} fusion(bf16[32,3,64,64]{3,2,0,1:T(8,128)(2,1)} %reshape.183, f32[32,3,64]{2,1,0:T(4,128)} %get-tuple-element.28, f32[32,3,64,66]{3,2,1,0:T(8,128)} %copy-done.3), kind=kOutput, calls=%fused_computation.27 | convolution fusion | flops 54343744 | bytes 3244032 | tf_op jit(solution)/shard_map/chlm,chle->cmhe/dot_general | solution.py:53
  199.9 3.6 %copy.82 = bf16[32,64,3,64]{1,0,3,2:T(8,128)(2,1)} copy(bf16[32,64,3,64]{1,3,2,0:T(8,128)(2,1)} %fusion.9) | data formatting | bytes 1572864 | tf_op jit(solution)/shard_map/convert_element_type | solution.py:64
  203.4 3.9 %reshape.184 = bf16[2048,192]{0,1:T(8,128)(2,1)} reshape(bf16[32,64,3,64]{1,0,3,2:T(8,128)(2,1)} %copy.82) | data formatting | bytes 1572864 | tf_op jit(solution)/shard_map/reshape | solution.py:70
  207.4 3.6 %copy.84 = bf16[32,66,3,64]{1,0,3,2:T(8,128)(2,1)} copy(bf16[32,66,3,64]{1,3,2,0:T(8,128)(2,1)} %fusion.10) | data formatting | bytes 1622016 | tf_op jit(solution)/shard_map/convert_element_type | solution.py:67
  210.9 4.2 %reshape.185 = bf16[2112,192]{0,1:T(8,128)(2,1)} reshape(bf16[32,66,3,64]{1,0,3,2:T(8,128)(2,1)} %copy.84) | data formatting | bytes 1622016 | tf_op jit(solution)/shard_map/reshape | solution.py:76
  215.1 2.9 fusion.52
  220.2 4.2 %reshape.186 = bf16[2112,192]{0,1:T(8,128)(2,1)} reshape(bf16[32,66,3,64]{1,0,3,2:T(8,128)(2,1)} %copy.86) | data formatting | bytes 1622016 | tf_op jit(solution)/shard_map/reshape | solution.py:82
  224.4 2.8 fusion.53
  235.2 2.7 fusion.51
  238.0 18.5 %reduce-scatter.4.cloned.1.call-done = bf16[192,64]{1,0:T(8,128)(2,1)} async-done(((bf16[768,64]{1,0:T(8,128)(2,1)}), bf16[192,64]{1,0:T(8,128)(2,1)}) %reduce-scatter.4.cloned.1.call-update) | async-done | bytes 24592
  260.9 5.7 %all-to-all-start.1 = ((bf16[192,8,256]{2,0,1:T(8,128)(2,1)}), bf16[192,8,256]{2,0,1:T(8,128)(2,1)S(1)}, u32[]{:S(2)}, u32[]{:S(2)}) async-start(bf16[192,8,256]{2,0,1:T(8,128)(2,1)} %bitcast.96), calls=%async_computation.1 | async-start | bytes 1572864 | tf_op jit(solution)/shard_map/all_to_all | solution.py:139
  266.6 14.6 %convolution_convert_fusion.7 = bf16[32,3,64,64]{3,2,1,0:T(8,128)(2,1)} fusion(bf16[32,66,3,64]{1,0,3,2:T(8,128)(2,1)S(1)} %copy-done.6, f32[32,3,64]{2,1,0:T(4,128)S(1)} %copy-done.8, f32[32,3,64,66]{3,2,1,0:T(8,128)} %copy-done.3), kind=kOutput, calls=%fused_computation.21 | convolution fusion | flops 54331456 | bytes 3244032 | tf_op jit(solution)/shard_map/chlm,cmhe->chle/dot_general | solution.py:46
  281.2 3.3 reshape.219
  286.0 5.4 %all-to-all-done.1 = bf16[192,8,256]{2,0,1:T(8,128)(2,1)S(1)} async-done(((bf16[192,8,256]{2,0,1:T(8,128)(2,1)}), bf16[192,8,256]{2,0,1:T(8,128)(2,1)S(1)}, u32[]{:S(2)}, u32[]{:S(2)}) %all-to-all-start.1) | async-done | bytes 786464 | tf_op jit(solution)/shard_map/all_to_all | solution.py:139
  293.6 12.5 %scatter_custom_fusion = f32[192,2048]{0,1:T(8,128)S(1)} fusion(s32[2048]{0:T(1024)S(1)} %bitcast.110, f32[2048,192]{1,0:T(8,128)} %copy.91, f32[]{:T(128)} %constant.12.clone.1), kind=kCustom, calls=%fused_computation.45 | custom fusion | flops 393216 | bytes 1573376 | tf_op jit(solution)/shard_map/scatter-add | solution.py:142
  307.7 32.4 %all-reduce.3.cloned.1.call-done = (f32[192,768]{1,0:T(8,128)}, f32[192,768]{1,0:T(8,128)}, f32[192,768]{1,0:T(8,128)}) async-done(((f32[192,768]{1,0:T(8,128)}, f32[192,768]{1,0:T(8,128)}, f32[192,768]{1,0:T(8,128)}), (f32[192,768]{1,0:T(8,128)}, f32[192,768]{1,0:T(8,128)}, f32[192,768]{1,0:T(8,128)})) %all-reduce.3.cloned.1.call-update) | async-done | bytes 1769488 | tf_op jit(solution)/shard_map/psum | solution.py:129
  (78 shorter events, 46.7 us)
Async XLA Ops:
  8.0 77.0 %copy-start = (bf16[192,768]{1,0:T(8,128)(2,1)S(1)}, bf16[192,768]{1,0:T(8,128)(2,1)}, u32[]{:S(2)}) copy-start(bf16[192,768]{1,0:T(8,128)(2,1)} %param.11) | copy-start | bytes 884740
  20.0 11.8 %copy-start.10 = (s32[32,2]{0,1:T(2,128)S(1)}, s32[32,2]{0,1:T(2,128)}, u32[]{:S(2)}) copy-start(s32[32,2]{0,1:T(2,128)} %param.17) | copy-start | bytes 772
  20.0 11.9 %copy-start.9 = (s32[32,2,32]{2,1,0:T(2,128)S(1)}, s32[32,2,32]{2,1,0:T(2,128)}, u32[]{:S(2)}) copy-start(s32[32,2,32]{2,1,0:T(2,128)} %param.16) | copy-start | bytes 24580
  20.0 12.3 %copy-start.11 = (s32[2]{0:T(128)S(1)}, s32[2]{0:T(128)}, u32[]{:S(2)}) copy-start(s32[2]{0:T(128)} %constant.31) | copy-start | bytes 28
  20.0 12.4 %copy-start.12 = (s32[2]{0:T(128)S(1)}, s32[2]{0:T(128)}, u32[]{:S(2)}) copy-start(s32[2]{0:T(128)} %constant.34) | copy-start | bytes 28
  20.0 26.7 %copy-start.1 = (bf16[32,64,768]{2,1,0:T(8,128)(2,1)S(1)}, bf16[32,64,768]{2,1,0:T(8,128)(2,1)}, u32[]{:S(2)}) copy-start(bf16[32,64,768]{2,1,0:T(8,128)(2,1)} %param.9) | copy-start | bytes 9437188
  24.5 32.2 %all-to-all-start = ((bf16[192,8,256]{2,0,1:T(8,128)(2,1)}), bf16[192,8,256]{2,0,1:T(8,128)(2,1)}, u32[]{:S(2)}, u32[]{:S(2)}) async-start(bf16[192,8,256]{2,0,1:T(8,128)(2,1)} %broadcast_select_fusion), calls=%async_computation | async-start | bytes 1572864 | tf_op jit(solution)/shard_map/all_to_all | solution.py:109
  31.7 224.8 %reduce-scatter.4.cloned.1.call-start = ((), (), s32[]{:S(2)}) async-start(), calls=%async_computation.3 | async-start | bytes 245760
  97.4 3.3 copy-start.3
  97.4 3.3 copy-start.5
  97.4 4.2 %copy-start.7 = (bf16[32,3,64,64]{3,2,0,1:T(8,128)(2,1)S(1)}, bf16[32,3,64,64]{3,2,0,1:T(8,128)(2,1)}, u32[]{:S(2)}) copy-start(bf16[32,3,64,64]{3,2,0,1:T(8,128)(2,1)} %reshape.183) | copy-start | bytes 2359300
  215.1 2.9 copy-start.4
  227.2 8.1 %copy-start.2 = (bf16[32,64,768]{2,1,0:T(8,128)(2,1)S(1)}, bf16[32,64,768]{2,1,0:T(8,128)(2,1)}, u32[]{:S(2)}) copy-start(bf16[32,64,768]{2,1,0:T(8,128)(2,1)} %param.9) | copy-start | bytes 9437188
  235.2 104.9 %all-reduce.3.cloned.1.call-start = ((), (), s32[]{:S(2)}) async-start(), calls=%async_computation.4 | async-start | bytes 3538944 | tf_op jit(solution)/shard_map/psum | solution.py:129
  238.0 28.6 %copy-start.6 = (bf16[32,66,3,64]{1,0,3,2:T(8,128)(2,1)S(1)}, bf16[32,66,3,64]{1,0,3,2:T(8,128)(2,1)}, u32[]{:S(2)}) copy-start(bf16[32,66,3,64]{1,0,3,2:T(8,128)(2,1)} %reshape.181) | copy-start | bytes 2433028
  238.0 28.7 %copy-start.8 = (f32[32,3,64]{2,1,0:T(4,128)S(1)}, f32[32,3,64]{2,1,0:T(4,128)}, u32[]{:S(2)}) copy-start(f32[32,3,64]{2,1,0:T(4,128)} %get-tuple-element.28) | copy-start | bytes 73732
  260.9 30.5 %all-to-all-start.1 = ((bf16[192,8,256]{2,0,1:T(8,128)(2,1)}), bf16[192,8,256]{2,0,1:T(8,128)(2,1)S(1)}, u32[]{:S(2)}, u32[]{:S(2)}) async-start(bf16[192,8,256]{2,0,1:T(8,128)(2,1)} %bitcast.96), calls=%async_computation.1 | async-start | bytes 1572864 | tf_op jit(solution)/shard_map/all_to_all | solution.py:139
Sparse Core Ops, SparseCore 0:
  235.3 21.1 reduce-scatter.3
Sparse Core Ops, SparseCore 1:
  240.1 100.0 all-reduce.2
where the time goes:
time: 359 us; the launch traced here: 353 us
  matrix products  139 us (39%)
  local copies, waits for them, and re-layouts  87.7 us (24%)
  waiting for transfers between devices  56.3 us (16%)
  other arithmetic  35.7 us (10%)
  between operations  15.9 us (4%)
  starting transfers between devices  13.1 us (4%)
  blocking collectives  5.59 us (2%)
    dot_general x1, matrix products, local_attend(): jnp.einsum('chlm,cmhe->clhe', score_low, keys, preferred_element_type=jnp...  39.9 us
    dot_general x1, matrix products, local_attend(): jnp.einsum('chlm,clhe->cmhe', score_low, queries, preferred_element_type=...  39.9 us
    psum x1, waiting for transfers between devices, body(): summed_weights = lax.psum((part_query, part_key, part_value), 'nodes')  32.4 us
    unnamed x3, waiting for transfers between devices  18.5 us
    dot_general x1, matrix products, local_attend(): jnp.einsum('chlm,chle->cmhe', probs_low, grad_heads, preferred_element_ty...  15.9 us
    dot_general x1, matrix products, local_attend(): jnp.einsum('chlm,cmhe->chle', probs_low, values, preferred_element_type=j...  14.6 us
    unnamed x36, local copies, waits for them, and re-layouts  13.4 us
    scatter-add x1, other arithmetic, body(): jnp.zeros((local_width, own_rows), jnp.float32).at[:, send_flat]  12.5 us
  transfers between devices with their start and end apart: 4, of which 3 were waited for; matrix products, arithmetic and copies ran while one was open for 19% of the time, Pallas kernels for 0%

commit v1 on v0

v1 whole, which is shorter than its diff:
```python
import functools
import math

import jax
import jax.numpy as jnp
from jax import lax
from jax.experimental import pallas as pl
from jax.experimental.pallas import tpu as pltpu
from jax.sharding import PartitionSpec as P

HD = 64
PAD = 16
LANES = 128
F32 = jnp.float32
BF16 = jnp.bfloat16
MESH = pl.DeviceIdType.MESH
VMEM_LIMIT = 56 * 1024 * 1024
ROWS_ROWS = (((1,), (1,)), ((), ()))
COLS_COLS = (((0,), (0,)), ((), ()))


def iota(shape, dim):
    return lax.broadcasted_iota(jnp.int32, shape, dim)


def ones_where(condition):
    return jnp.where(condition, 1.0, 0.0).astype(BF16)


def send(src, dst, sems, slot, axis, peer):
    return pltpu.make_async_remote_copy(
        src_ref=src,
        dst_ref=dst,
        send_sem=sems.at[0, slot],
        recv_sem=sems.at[1, slot],
        device_id={axis: peer},
        device_id_type=MESH,
    )


def greet(n, m, me, my):
    barrier = pltpu.get_barrier_semaphore()

    def hail(axis, size, here):
        def one(step, carry):
            pl.semaphore_signal(
                barrier, inc=1, device_id={axis: lax.rem(here + step, size)}, device_id_type=MESH
            )
            return carry

        lax.fori_loop(1, size, one, 0)

    hail("nodes", n, me)
    hail("mp", m, my)
    pl.semaphore_wait(barrier, n + m - 2)


def each(size, action):
    def one(step, carry):
        action(step)
        return carry

    lax.fori_loop(1, size, one, 0)


def fetch_kernel(
    n, m, cls_ref, send_ref, slot_ref, count_ref, virt_ref, mix_ref,
    slots, parts, arrived, cols, slot_sems, part_sems, col_sems,
):
    me, my = lax.axis_index("nodes"), lax.axis_index("mp")
    rows = cls_ref.shape[1]
    slot_width, pairs = slot_ref.shape
    cap = send_ref.shape[2] // 2
    greet(n, m, me, my)

    def slot_copy(step):
        return send(slot_ref, slots.at[me], slot_sems, step, "nodes", lax.rem(me + step, n))

    each(n, lambda step: slot_copy(step).start())
    slots[pl.ds(me, 1)] = slot_ref[...][None]
    each(n, lambda step: slot_copy(step).wait())

    chunk = 256
    lane = iota((cap, 2 * pairs), 1)

    def group(g, carry):
        wanted = jnp.concatenate([slots[2 * g], slots[2 * g + 1]], axis=1)
        target = iota((cap, 2 * pairs), 0) + me * cap
        total = jnp.zeros((cap, 2 * pairs), F32)
        for k in range(slot_width):
            total = total + jnp.where(target == wanted[k : k + 1, :], 1.0, 0.0)
        mixed = jnp.concatenate(
            [jnp.where(lane < pairs, total, 0.0), jnp.where(lane >= pairs, total, 0.0)], axis=0
        ).astype(BF16)
        chosen = send_ref[g]
        for r in range(0, rows, chunk):
            hot = ones_where(iota((chunk, 2 * cap), 0) + r == chosen)
            mix_ref[g, r : r + chunk, :] = jnp.dot(
                hot, mixed, preferred_element_type=F32
            ).astype(BF16)
        part = jnp.dot(cls_ref[...], mix_ref[g], preferred_element_type=F32)
        turned = part.T
        parts[2 * g] = turned[:pairs]
        parts[2 * g + 1] = turned[pairs:]
        return carry

    lax.fori_loop(0, n // 2, group, 0)

    def part_copy(step):
        peer = lax.rem(me + step, n)
        return send(parts.at[peer], arrived.at[me], part_sems, step, "nodes", peer)

    each(n, lambda step: part_copy(step).start())
    arrived[pl.ds(me, 1)] = parts[pl.ds(me, 1)]
    each(n, lambda step: part_copy(step).wait())
    total = arrived[0]
    for b in range(1, n):
        total = total + arrived[b]
    cols[pl.ds(my, 1)] = (total / count_ref[...]).astype(BF16)[None]

    def col_copy(step):
        return send(
            cols.at[my], cols.at[my], col_sems, step, "mp", lax.rem(my + step, m)
        )

    each(m, lambda step: col_copy(step).start())
    each(m, lambda step: col_copy(step).wait())
    virt_ref[...] = cols[...]


def fetch(n, m, owned_cls, send_rows, slots_t, counts):
    width, rows = owned_cls.shape
    cap = send_rows.shape[1]
    slot_width, pairs = slots_t.shape
    vmem = pl.BlockSpec(memory_space=pltpu.VMEM)
    return pl.pallas_call(
        functools.partial(fetch_kernel, n, m),
        out_shape=(
            jax.ShapeDtypeStruct((m, pairs, width), BF16),
            jax.ShapeDtypeStruct((n // 2, rows, 2 * pairs), BF16),
        ),
        in_specs=[vmem] * 4,
        out_specs=(vmem, vmem),
        scratch_shapes=[
            pltpu.VMEM((n, slot_width, pairs), jnp.int32),
            pltpu.VMEM((n, pairs, width), F32),
            pltpu.VMEM((n, pairs, width), F32),
            pltpu.VMEM((m, pairs, width), BF16),
            pltpu.SemaphoreType.DMA((2, n)),
            pltpu.SemaphoreType.DMA((2, n)),
            pltpu.SemaphoreType.DMA((2, m)),
        ],
        compiler_params=pltpu.CompilerParams(
            collective_id=1, has_side_effects=True, vmem_limit_bytes=VMEM_LIMIT
        ),
        name="fetch",
    )(owned_cls, send_rows.reshape(n // 2, 1, 2 * cap), slots_t, counts)


def attend_kernel(
    types, virt_ref, tok_ref, wq_ref, wk_ref, wv_ref, g_ref, ctx_ref, wsum_ref, vg_ref,
    tok, vpad, qs, ks, vs, kv, vv, dq, dk, dv, dkv, dvv,
):
    m, pairs, share = virt_ref.shape
    heads, centres, half, _ = g_ref.shape
    length = 2 * half
    width = heads * HD
    model = tok_ref.shape[1]
    span = length + PAD
    wide = heads * length

    spread_row = iota((centres * PAD, pairs), 0)
    spread = ones_where(
        ((spread_row // PAD) * types + spread_row % PAD == iota((centres * PAD, pairs), 1))
        & (spread_row % PAD < types)
    )
    virt = jnp.concatenate([virt_ref[i].astype(F32) for i in range(m)], axis=1).astype(BF16)
    vpad[...] = jnp.dot(spread, virt, preferred_element_type=F32).astype(BF16)
    kv[...] = lax.dot_general(
        vpad[...], wk_ref[...], ROWS_ROWS, preferred_element_type=F32
    ).astype(BF16)
    vv[...] = lax.dot_general(
        vpad[...], wv_ref[...], ROWS_ROWS, preferred_element_type=F32
    ).astype(BF16)

    block = 4 * length
    to_row, from_row = iota((block, block), 0), iota((block, block), 1)
    inside = to_row % length
    swap = ones_where(
        from_row == (to_row - inside) + jnp.where(inside < half, 2 * inside, 2 * (inside - half) + 1)
    )

    def project(i, carry):
        here = pl.ds(pl.multiple_of(i * block, block), block)
        rows = jnp.dot(swap, tok_ref[here, :], preferred_element_type=F32).astype(BF16)
        tok[here, :] = rows
        for w_ref, out in ((wq_ref, qs), (wk_ref, ks), (wv_ref, vs)):
            out[here, :] = lax.dot_general(
                rows, w_ref[...], ROWS_ROWS, preferred_element_type=F32
            ).astype(BF16)
        return carry

    lax.fori_loop(0, centres * length // block, project, 0)

    scale = 1.0 / math.sqrt(HD)
    lane_head = iota((1, width), 1) // HD
    head_lanes = [ones_where(lane_head == h) for h in range(heads)]
    own = jnp.where(
        iota((wide, width), 0) // length == iota((wide, width), 1) // HD, 1.0, 0.0
    )
    pair_lane = iota((1, 2 * HD), 1)
    left, right = ones_where(pair_lane < HD), ones_where(pair_lane >= HD)
    copies = ones_where(iota((2 * HD, width), 0) % HD == iota((2 * HD, width), 1) % HD)
    live = iota((span, wide), 0) < length + types

    def one(c):
        text = pl.ds(pl.multiple_of(c * length, length), length)
        extra = pl.ds(pl.multiple_of(c * PAD, PAD), PAD)
        q = qs[text, :]
        q_diag = jnp.concatenate([q * lanes for lanes in head_lanes], axis=0)
        k = jnp.concatenate([ks[text, :], kv[extra, :]], axis=0)
        v = jnp.concatenate([vs[text, :], vv[extra, :]], axis=0)
        g_rows = []
        for h in range(heads):
            block_g = g_ref[h, c]
            g_rows += [block_g * left, block_g * right]
        g_diag = (
            jnp.dot(jnp.concatenate(g_rows, axis=0), copies, preferred_element_type=F32) * own
        ).astype(BF16)
        scores = lax.dot_general(k, q_diag, ROWS_ROWS, preferred_element_type=F32) * scale
        scores = jnp.where(live, scores, -jnp.inf)
        grown = jnp.exp(scores - jnp.max(scores, axis=0, keepdims=True))
        probs = grown / jnp.sum(grown, axis=0, keepdims=True)
        low = probs.astype(BF16)
        prob_grads = lax.dot_general(v, g_diag, ROWS_ROWS, preferred_element_type=F32)
        dots = jnp.sum(prob_grads * probs, axis=0, keepdims=True)
        score_low = (probs * (prob_grads - dots) * scale).astype(BF16)
        dv_all = jnp.dot(low, g_diag, preferred_element_type=F32).astype(BF16)
        dk_all = jnp.dot(score_low, q_diag, preferred_element_type=F32).astype(BF16)
        dv[text, :], dvv[extra, :] = dv_all[:length], dv_all[length:]
        dk[text, :], dkv[extra, :] = dk_all[:length], dk_all[length:]
        out = (lax.dot_general(low, v, COLS_COLS, preferred_element_type=F32) * own).astype(BF16)
        flat = lax.dot_general(out, copies, ROWS_ROWS, preferred_element_type=F32)
        for h in range(heads):
            at = h * length
            ctx_ref[h, c] = jnp.where(
                pair_lane < HD, flat[at : at + half], flat[at + half : at + length]
            ).astype(BF16)
        dq_all = lax.dot_general(score_low, k, COLS_COLS, preferred_element_type=F32) * own
        dq_sum = dq_all[:length]
        for h in range(1, heads):
            dq_sum = dq_sum + dq_all[h * length : (h + 1) * length]
        dq[text, :] = dq_sum.astype(BF16)

    def several(i, carry):
        for j in range(UNROLL):
            one(i * UNROLL + j)
        return carry

    lax.fori_loop(0, centres // UNROLL, several, 0)

    part_q = lax.dot_general(dq[...], tok[...], COLS_COLS, preferred_element_type=F32)
    part_k = lax.dot_general(
        dk[...], tok[...], COLS_COLS, preferred_element_type=F32
    ) + lax.dot_general(dkv[...], vpad[...], COLS_COLS, preferred_element_type=F32)
    part_v = lax.dot_general(
        dv[...], tok[...], COLS_COLS, preferred_element_type=F32
    ) + lax.dot_general(dvv[...], vpad[...], COLS_COLS, preferred_element_type=F32)
    at = 0
    for part in (part_q, part_k, part_v):
        for lanes in range(0, model, LANES):
            wsum_ref[at : at + width, :] = part[:, lanes : lanes + LANES].astype(BF16)
            at += width
    if at < wsum_ref.shape[0]:
        wsum_ref[at:, :] = jnp.zeros((wsum_ref.shape[0] - at, LANES), BF16)
    few_k = lax.dot_general(spread, dkv[...], COLS_COLS, preferred_element_type=F32).astype(BF16)
    few_v = lax.dot_general(spread, dvv[...], COLS_COLS, preferred_element_type=F32).astype(BF16)
    vg = jnp.dot(few_k, wk_ref[...], preferred_element_type=F32) + jnp.dot(
        few_v, wv_ref[...], preferred_element_type=F32
    )
    for i in range(m):
        vg_ref[i] = vg[:, i * share : (i + 1) * share]


UNROLL = 2


def attend(total_rows, types, virt, tokens, w_query, w_key, w_value, grads):
    m, pairs, share = virt.shape
    heads, centres, half, _ = grads.shape
    count, model = tokens.shape
    width = heads * HD
    vmem = pl.BlockSpec(memory_space=pltpu.VMEM)
    extra = centres * PAD
    narrow, small = pltpu.VMEM((count, width), BF16), pltpu.VMEM((extra, width), BF16)
    return pl.pallas_call(
        functools.partial(attend_kernel, types),
        out_shape=(
            jax.ShapeDtypeStruct(grads.shape, BF16),
            jax.ShapeDtypeStruct((total_rows, LANES), BF16),
            jax.ShapeDtypeStruct((m, pairs, share), F32),
        ),
        in_specs=[vmem] * 6,
        out_specs=(vmem, vmem, vmem),
        scratch_shapes=[
            pltpu.VMEM((count, model), BF16), pltpu.VMEM((extra, model), BF16),
            narrow, narrow, narrow, small, small, narrow, narrow, narrow, small, small,
        ],
        compiler_params=pltpu.CompilerParams(vmem_limit_bytes=VMEM_LIMIT),
        name="attend",
    )(virt, tokens, w_query, w_key, w_value, grads)


def reduce_kernel(
    n, m, wsum_ref, vg_ref, count_ref, weights_ref, shared_ref,
    w_in, w_all, vg_in, shared, vg_sems, sh_sems, rs_sems, ag_sems,
):
    me, my = lax.axis_index("nodes"), lax.axis_index("mp")
    chunk = w_in.shape[1]
    greet(n, m, me, my)

    def vg_copy(step):
        peer = lax.rem(my + step, m)
        return send(vg_ref.at[peer], vg_in.at[my], vg_sems, step, "mp", peer)

    def rs_copy(step):
        peer = lax.rem(me + step, n)
        return send(wsum_ref.at[peer], w_in.at[me], rs_sems, step, "nodes", peer)

    def sh_copy(step):
        return send(shared.at[me], shared.at[me], sh_sems, step, "nodes", lax.rem(me + step, n))

    def ag_copy(step):
        return send(w_all.at[me], w_all.at[me], ag_sems, step, "nodes", lax.rem(me + step, n))

    each(m, lambda step: vg_copy(step).start())
    each(n, lambda step: rs_copy(step).start())
    vg_in[pl.ds(my, 1)] = vg_ref[pl.ds(my, 1)]
    w_in[pl.ds(me, 1)] = wsum_ref[pl.ds(me, 1)]
    each(m, lambda step: vg_copy(step).wait())
    total = vg_in[0]
    for i in range(1, m):
        total = total + vg_in[i]
    shared[pl.ds(me, 1)] = (total / count_ref[...]).astype(BF16)[None]
    each(n, lambda step: sh_copy(step).start())
    each(n, lambda step: rs_copy(step).wait())
    weights = w_in[0].astype(F32)
    for b in range(1, n):
        weights = weights + w_in[b].astype(F32)
    w_all[pl.ds(me, 1)] = weights.astype(BF16)[None]
    each(n, lambda step: ag_copy(step).start())
    each(n, lambda step: sh_copy(step).wait())
    shared_ref[...] = shared[...]
    each(n, lambda step: ag_copy(step).wait())
    weights_ref[...] = w_all[...]


def reduce_all(n, m, wsum, vg, counts):
    chunk = wsum.shape[0] // n
    _, pairs, share = vg.shape
    vmem = pl.BlockSpec(memory_space=pltpu.VMEM)
    return pl.pallas_call(
        functools.partial(reduce_kernel, n, m),
        out_shape=(
            jax.ShapeDtypeStruct((n, chunk, LANES), BF16),
            jax.ShapeDtypeStruct((n, pairs, share), BF16),
        ),
        in_specs=[vmem] * 3,
        out_specs=(vmem, vmem),
        scratch_shapes=[
            pltpu.VMEM((n, chunk, LANES), BF16),
            pltpu.VMEM((n, chunk, LANES), BF16),
            pltpu.VMEM((m, pairs, share), F32),
            pltpu.VMEM((n, pairs, share), BF16),
            pltpu.SemaphoreType.DMA((2, m)),
            pltpu.SemaphoreType.DMA((2, n)),
            pltpu.SemaphoreType.DMA((2, n)),
            pltpu.SemaphoreType.DMA((2, n)),
        ],
        compiler_params=pltpu.CompilerParams(
            collective_id=2, has_side_effects=True, vmem_limit_bytes=VMEM_LIMIT
        ),
        name="reduce",
    )(wsum.reshape(n, chunk, LANES), vg, counts)


def finish_kernel(weights_ref, shared_ref, mix_ref, q_ref, k_ref, v_ref, cls_ref):
    width, model = q_ref.shape
    groups = mix_ref.shape[0]
    at = 0
    for out in (q_ref, k_ref, v_ref):
        for lanes in range(0, model, LANES):
            out[:, lanes : lanes + LANES] = weights_ref[at : at + width, :].astype(F32)
            at += width

    def group(g, carry):
        both = jnp.concatenate([shared_ref[2 * g], shared_ref[2 * g + 1]], axis=0)
        turned = both.astype(F32).T.astype(BF16)
        part = lax.dot_general(turned, mix_ref[g], ROWS_ROWS, preferred_element_type=F32)

        @pl.when(g == 0)
        def _():
            cls_ref[...] = part

        @pl.when(g > 0)
        def _():
            cls_ref[...] += part

        return carry

    lax.fori_loop(0, groups, group, 0)


def finish(weights, shared, mix, width, model):
    vmem = pl.BlockSpec(memory_space=pltpu.VMEM)
    weight = jax.ShapeDtypeStruct((width, model), F32)
    rows = mix.shape[1]
    return pl.pallas_call(
        finish_kernel,
        out_shape=(weight, weight, weight, jax.ShapeDtypeStruct((shared.shape[2], rows), F32)),
        in_specs=[vmem] * 3,
        out_specs=(vmem,) * 4,
        compiler_params=pltpu.CompilerParams(vmem_limit_bytes=VMEM_LIMIT),
        name="finish",
    )(weights, shared, mix)


def body(n, m, tokens, w_query, w_key, w_value, grad_out, owned_cls, send_rows, neigh_slot, neigh_count):
    centres, length, model = tokens.shape
    width = w_query.shape[0]
    heads = width // HD
    types, slot_width = neigh_slot.shape[1:]
    pairs = centres * types
    live = lax.broadcasted_iota(jnp.int32, neigh_slot.shape, 2) < neigh_count[:, :, None]
    slots_t = jnp.where(live, neigh_slot, -1).reshape(pairs, slot_width).T
    counts = neigh_count.reshape(pairs, 1).astype(F32)
    virt, mix = fetch(n, m, owned_cls, send_rows[0], slots_t, counts)
    grads = grad_out.transpose(1, 0, 2).reshape(heads, centres, length // 2, 2 * HD)
    pieces = 3 * width * (model // LANES)
    chunk = -(-pieces // (n * 16)) * 16
    context, wsum, vg = attend(
        n * chunk, types, virt, tokens.reshape(-1, model), w_query, w_key, w_value, grads
    )
    weights, shared = reduce_all(n, m, wsum, vg, counts)
    grad_q, grad_k, grad_v, grad_cls = finish(
        weights.reshape(n * chunk, LANES), shared, mix, width, model
    )
    context = context.reshape(heads, centres, length * HD).transpose(1, 0, 2)
    return context, grad_q, grad_k, grad_v, grad_cls


def solution(mesh):
    in_specs = (
        P("nodes", None, None),
        P("mp", None),
        P("mp", None),
        P("mp", None),
        P("nodes", "mp", None),
        P("mp", "nodes"),
        P("nodes", None, None),
        P("nodes", None, None),
        P("nodes", None),
    )
    out_specs = (
        P("nodes", "mp", None),
        P("mp", None),
        P("mp", None),
        P("mp", None),
        P("mp", "nodes"),
    )
    return jax.shard_map(
        functools.partial(body, mesh.shape["nodes"], mesh.shape["mp"]),
        mesh=mesh, in_specs=in_specs, out_specs=out_specs, check_vma=False,
    )
```

time: 359 us -> 128 us (0.36); the launches traced: 353 us -> 126 us
  matrix products: 139 us -> 0 us
  Pallas kernels: 0 us -> 116 us
  local copies, waits for them, and re-layouts: 87.7 us -> 7.84 us
  waiting for transfers between devices: 56.3 us -> 0 us
  other arithmetic: 35.7 us -> 1.54 us
  between operations: 15.9 us -> 0.66 us
  starting transfers between devices: 13.1 us -> 0 us
  blocking collectives: 5.59 us -> 0 us
    dot_general x16 -> x0, matrix products: 139 us -> none  [the longest x1 39.9 us: local_attend(): jnp.einsum('chlm,cmhe->clhe', score_low, keys, preferred_element_type=jnp...]
    pallas_call x0 -> x4, Pallas kernels: none -> 116 us  [the longest x1 49.7 us: reduce_all(): pl.pallas_call(functools.partial(reduce_kernel, n, m), out_shape=(jax.Sha...]
    reshape x15 -> x2, local copies, waits for them, and re-layouts: 42.2 us -> 2.83 us  [the longest x1 2.15 us: body(): context = context.reshape(heads, centres, length * HD).transpose(1, 0, 2)]
    psum x1 -> x0, waiting for transfers between devices: 32.4 us -> none  [body(): summed_weights = lax.psum((part_query, part_key, part_value), 'nodes')]
    unnamed x3 -> x0, waiting for transfers between devices: 18.5 us -> none
    all_to_all x2 -> x0, starting transfers between devices: 13 us -> none  [the longest x1 7.25 us: body(): lax.all_to_all(outgoing, 'nodes', split_axis=1, concat_axis=1, tiled=True)]
    scatter-add x1 -> x0, other arithmetic: 12.5 us -> none  [body(): jnp.zeros((local_width, own_rows), jnp.float32).at[:, send_flat]]
    unnamed x5 -> x0, other arithmetic: 12.4 us -> none
  transfers between devices with their start and end apart: 4 -> 0, of which waited for: 3 -> 0; matrix products, arithmetic and copies ran while one was open for 19% -> 0% of each run, Pallas kernels for 0% -> 0%
where the time goes in v1:
time: 128 us; the launch traced here: 126 us
  Pallas kernels  116 us (91%)
  local copies, waits for them, and re-layouts  7.84 us (6%)
  other arithmetic  1.54 us (1%)
    pallas_call x1, Pallas kernels, reduce_all(): pl.pallas_call(functools.partial(reduce_kernel, n, m), out_shape=(jax.Sha...  49.7 us
    pallas_call x1, Pallas kernels, fetch(): pl.pallas_call(functools.partial(fetch_kernel, n, m), out_shape=(jax.Shap...  32.5 us
    pallas_call x1, Pallas kernels, attend(): pl.pallas_call(functools.partial(attend_kernel, types), out_shape=(jax.Sh...  28.2 us
    pallas_call x1, Pallas kernels, finish(): pl.pallas_call(finish_kernel, out_shape=(weight, weight, weight, jax.Shap...  5.94 us
    unnamed x2, local copies, waits for them, and re-layouts  2.93 us

profile of v1, /device:TPU:0, one launch (start us, length us, event | category | flops | bytes accessed | tf_op | source)
XLA Modules:
  0.0 126.4 jit_solution(14937695965514108660)
XLA Ops:
  0.6 0.7 convert_element_type.5
  1.3 1.3 %reshape_squeeze.3.send_ref = s32[4,1,512]{2,1,0:T(1,128)} reshape(s32[1,8,256]{2,1,0:T(8,128)} %param.15) | data formatting | bytes 16384 | tf_op jit(solution)/shard_map/reshape;squeeze | solution.py:157
  2.6 0.1 copy.21
  2.7 0.7 convert_element_type.7.count_ref
  3.4 0.8 copy.19
  4.2 0.9 compare_select_fusion
  5.0 0.7 copy.20
  5.7 2.2 %copy.24 = bf16[12,8,32,128]{3,2,1,0:T(8,128)(2,1)} copy(bf16[12,8,32,128]{3,1,2,0:T(8,128)(2,1)} %bitcast.17) | data formatting | bytes 1572864
  7.9 32.5 %fetch.1 = (bf16[4,64,192]{2,1,0:T(8,128)(2,1)}, bf16[4,2048,128]{2,1,0:T(8,128)(2,1)}) custom-call(bf16[192,2048]{1,0:T(8,128)(2,1)} %cls_ref.1, s32[4,1,512]{2,1,0:T(1,128)} %reshape_squeeze.3.send_ref, s32[32,64]{1,0:T(8,128)} %bitcast.20, f32[64,1]{1,0:T(8,128)} %convert_element_type.7.count_ref), custom_call_target="tpu_custom_call" | custom-call | tf_op jit(solution)/shard_map/fetch/pallas_call | solution.py:136
  40.4 28.2 %attend.1 = (bf16[3,32,32,128]{3,2,1,0:T(8,128)(2,1)}, bf16[3456,128]{1,0:T(8,128)(2,1)}, f32[4,64,192]{2,1,0:T(8,128)}) custom-call(bf16[4,64,192]{2,1,0:T(8,128)(2,1)} %get-tuple-element.16.virt_ref, bf16[2048,768]{1,0:T(8,128)(2,1)} %bitcast.14, bf16[192,768]{1,0:T(8,128)(2,1)} %wq_ref.1, bf16[192,768]{1,0:T(8,128)(2,1)} %wk_ref.1, ...), custom_call_target="tpu_custom_call" | custom-call | tf_op jit(solution)/shard_map/attend/pallas_call | solution.py:296
  68.6 2.1 %reshape.46 = bf16[3,32,4096]{2,1,0:T(8,128)(2,1)} reshape(bf16[3,32,32,128]{3,2,1,0:T(8,128)(2,1)} %get-tuple-element.17) | data formatting | bytes 1572864 | tf_op jit(solution)/shard_map/reshape | solution.py:448
  70.8 49.7 %reduce.1 = (bf16[8,432,128]{2,1,0:T(8,128)(2,1)}, bf16[8,64,192]{2,1,0:T(8,128)(2,1)}) custom-call(bf16[8,432,128]{2,1,0:T(8,128)(2,1)} %bitcast.16, f32[4,64,192]{2,1,0:T(8,128)} %get-tuple-element.19.vg_ref, f32[64,1]{1,0:T(8,128)} %convert_element_type.7.count_ref), custom_call_target="tpu_custom_call" | custom-call | tf_op jit(solution)/shard_map/reduce/pallas_call | solution.py:362
  120.5 5.9 %finish.1 = (f32[192,768]{1,0:T(8,128)}, f32[192,768]{1,0:T(8,128)}, f32[192,768]{1,0:T(8,128)}, f32[192,2048]{1,0:T(8,128)}) custom-call(bf16[3456,128]{1,0:T(8,128)(2,1)} %bitcast.15, bf16[8,64,192]{2,1,0:T(8,128)(2,1)} %get-tuple-element.21.shared_ref, bf16[4,2048,128]{2,1,0:T(8,128)(2,1)} %get-tuple-element.22.mix_ref), custom_call_target="tpu_custom_call" | custom-call | tf_op jit(solution)/shard_map/finish/pallas_call | solution.py:418

commit v2 on v1

v2 whole, which is shorter than its diff:
```python
import functools
import math

import jax
import jax.numpy as jnp
from jax import lax
from jax.experimental import pallas as pl
from jax.experimental.pallas import tpu as pltpu
from jax.sharding import PartitionSpec as P

HD = 64
PAD = 16
LANES = 128
F32 = jnp.float32
BF16 = jnp.bfloat16
MESH = pl.DeviceIdType.MESH
VMEM_LIMIT = 56 * 1024 * 1024
ROWS_ROWS = (((1,), (1,)), ((), ()))
COLS_COLS = (((0,), (0,)), ((), ()))


def iota(shape, dim):
    return lax.broadcasted_iota(jnp.int32, shape, dim)


def ones_where(condition):
    return jnp.where(condition, 1.0, 0.0).astype(BF16)


def send(src, dst, sems, slot, axis, peer):
    return pltpu.make_async_remote_copy(
        src_ref=src,
        dst_ref=dst,
        send_sem=sems.at[(0, *slot)],
        recv_sem=sems.at[(1, *slot)],
        device_id={axis: peer},
        device_id_type=MESH,
    )


def greet(n, m, me, my):
    barrier = pltpu.get_barrier_semaphore()

    def hail(axis, size, here):
        def one(step, carry):
            pl.semaphore_signal(
                barrier, inc=1, device_id={axis: lax.rem(here + step, size)}, device_id_type=MESH
            )
            return carry

        lax.fori_loop(1, size, one, 0)

    hail("nodes", n, me)
    hail("mp", m, my)
    pl.semaphore_wait(barrier, n + m - 2)


def each(size, action):
    def one(step, carry):
        action(step)
        return carry

    lax.fori_loop(1, size, one, 0)


UNROLL = 2


def layer_kernel(
    n, m, types,
    tok_ref, wq_ref, wk_ref, wv_ref, g_ref, cls_ref, send_ref, slot_ref, count_ref,
    ctx_ref, weights_ref, shared_ref, mix_ref,
    slots_own, slots, parts, arrived, cols,
    tok, vpad, qs, ks, vs, kv, vv, dq, dk, dv, dkv, dvv, lows,
    wsum, x_in, z_sum, z_in, w_all, vg_out, vg_in, shared,
    slot_sems, part_sems, col_sems, vg_sems, sh_sems, x_sems, z_sems, a_sems, f_sems,
):
    me, my = lax.axis_index("nodes"), lax.axis_index("mp")
    zs = n // 2
    par, zz = lax.rem(me, 2), lax.div(me, 2)
    mate = me + 1 - 2 * par
    rows = cls_ref.shape[1]
    cap = send_ref.shape[1]
    centres, _, slot_width = slot_ref.shape
    pairs = centres * types
    heads, _, half, _ = g_ref.shape
    length = 2 * half
    width = heads * HD
    model = tok_ref.shape[1]
    share = model // m
    span = length + PAD
    wide = heads * length

    counts = count_ref[...].astype(F32)
    lists = []
    for t in range(types):
        turned = slot_ref[:, t, :].astype(F32).T
        spot = iota((slot_width, centres), 0).astype(F32)
        lists.append(jnp.where(spot < counts[t : t + 1, :], turned, -1.0))
    slots_own[...] = jnp.concatenate(lists, axis=1)
    count_row = jnp.concatenate([counts[t : t + 1, :] for t in range(types)], axis=1)
    count_col = jnp.broadcast_to(count_row, (8, pairs)).T[:, :1]

    greet(n, m, me, my)

    def slot_copy(step):
        return send(slots_own, slots.at[me], slot_sems, (step,), "nodes", lax.rem(me + step, n))

    each(n, lambda step: slot_copy(step).start())
    slots[pl.ds(me, 1)] = slots_own[...][None]

    block = 4 * length
    to_row, from_row = iota((block, block), 0), iota((block, block), 1)
    inside = to_row % length
    swap = ones_where(
        from_row == (to_row - inside) + jnp.where(inside < half, 2 * inside, 2 * (inside - half) + 1)
    )

    def project(i, carry):
        here = pl.ds(pl.multiple_of(i * block, block), block)
        moved = jnp.dot(swap, tok_ref[here, :], preferred_element_type=F32).astype(BF16)
        tok[here, :] = moved
        for w_ref, out in ((wq_ref, qs), (wk_ref, ks), (wv_ref, vs)):
            out[here, :] = lax.dot_general(
                moved, w_ref[...], ROWS_ROWS, preferred_element_type=F32
            ).astype(BF16)
        return carry

    blocks = centres * length // block
    lax.fori_loop(0, blocks // 2, project, 0)
    each(n, lambda step: slot_copy(step).wait())

    chunk = 256
    lane = iota((cap, 2 * pairs), 1)
    target = (iota((cap, 2 * pairs), 0) + me * cap).astype(F32)

    def group(g, carry):
        wanted = jnp.concatenate([slots[2 * g], slots[2 * g + 1]], axis=1)
        total = jnp.zeros((cap, 2 * pairs), F32)
        for k in range(slot_width):
            total = total + jnp.where(target == wanted[k : k + 1, :], 1.0, 0.0)
        mixed = jnp.concatenate(
            [jnp.where(lane < pairs, total, 0.0), jnp.where(lane >= pairs, total, 0.0)], axis=0
        ).astype(BF16)
        chosen = jnp.concatenate(
            [send_ref[pl.ds(2 * g, 1), :], send_ref[pl.ds(2 * g + 1, 1), :]], axis=1
        )
        for r in range(0, rows, chunk):
            hot = ones_where(iota((chunk, 2 * cap), 0) + r == chosen)
            mix_ref[g, r : r + chunk, :] = jnp.dot(
                hot, mixed, preferred_element_type=F32
            ).astype(BF16)
        turned = jnp.dot(cls_ref[...], mix_ref[g], preferred_element_type=F32).T
        parts[2 * g] = turned[:pairs]
        parts[2 * g + 1] = turned[pairs:]
        return carry

    lax.fori_loop(0, n // 2, group, 0)

    def part_copy(step):
        peer = lax.rem(me + step, n)
        return send(parts.at[peer], arrived.at[me], part_sems, (step,), "nodes", peer)

    each(n, lambda step: part_copy(step).start())
    arrived[pl.ds(me, 1)] = parts[pl.ds(me, 1)]
    lax.fori_loop(blocks // 2, blocks, project, 0)
    each(n, lambda step: part_copy(step).wait())
    total = arrived[0]
    for b in range(1, n):
        total = total + arrived[b]
    cols[pl.ds(my, 1)] = (total / count_col).astype(BF16)[None]

    def col_copy(step):
        return send(cols.at[my], cols.at[my], col_sems, (step,), "mp", lax.rem(my + step, m))

    each(m, lambda step: col_copy(step).start())
    spread_row = iota((centres * PAD, pairs), 0)
    spread = ones_where(
        ((spread_row % PAD) * centres + spread_row // PAD == iota((centres * PAD, pairs), 1))
        & (spread_row % PAD < types)
    )
    each(m, lambda step: col_copy(step).wait())
    virt = jnp.concatenate([cols[i].astype(F32) for i in range(m)], axis=1).astype(BF16)
    vpad[...] = jnp.dot(spread, virt, preferred_element_type=F32).astype(BF16)
    kv[...] = lax.dot_general(
        vpad[...], wk_ref[...], ROWS_ROWS, preferred_element_type=F32
    ).astype(BF16)
    vv[...] = lax.dot_general(
        vpad[...], wv_ref[...], ROWS_ROWS, preferred_element_type=F32
    ).astype(BF16)

    def x_copy(p):
        return send(wsum.at[p, 1 - par], x_in.at[p], x_sems, (p,), "nodes", mate)

    def z_copy(p, step):
        peer = lax.rem(zz + step, zs)
        return send(z_sum.at[p, peer], z_in.at[p, zz], z_sems, (p, step), "nodes", 2 * peer + par)

    def a_copy(p, step):
        own = w_all.at[p, par, zz]
        return send(own, own, a_sems, (p, step), "nodes", 2 * lax.rem(zz + step, zs) + par)

    def f_copy(p, step):
        held = w_all.at[p, par, lax.rem(zz - step + zs, zs)]
        return send(held, held, f_sems, (p, step), "nodes", mate)

    def part_ready(p, part):
        at = 0
        flat = []
        for lanes in range(0, model, LANES):
            flat.append(part[:, lanes : lanes + LANES].astype(BF16))
        flat = jnp.concatenate(flat, axis=0)
        _, _, _, size, _ = wsum.shape
        short = 2 * zs * size - flat.shape[0]
        if short:
            flat = jnp.concatenate([flat, jnp.zeros((short, LANES), BF16)], axis=0)
        wsum[p] = flat.reshape(2, zs, size, LANES)
        x_copy(p).start()

    def x_done(p):
        x_copy(p).wait()
        z_sum[p] = (wsum[p, par].astype(F32) + x_in[p].astype(F32)).astype(BF16)
        each(zs, lambda step: z_copy(p, step).start())
        z_in[p, pl.ds(zz, 1)] = z_sum[p, pl.ds(zz, 1)]

    def z_done(p):
        each(zs, lambda step: z_copy(p, step).wait())
        weights = z_in[p, 0].astype(F32)
        for b in range(1, zs):
            weights = weights + z_in[p, b].astype(F32)
        w_all[p, par, zz] = weights.astype(BF16)
        each(zs, lambda step: a_copy(p, step).start())
        f_copy(p, 0).start()

    def a_done(p):
        def forward(step):
            a_copy(p, step).wait()
            f_copy(p, step).start()

        each(zs, forward)

    def f_done(p):
        f_copy(p, 0).wait()
        each(zs, lambda step: f_copy(p, step).wait())

    scale = 1.0 / math.sqrt(HD)
    lane_head = iota((1, width), 1) // HD
    head_lanes = [ones_where(lane_head == h) for h in range(heads)]
    own = jnp.where(
        iota((wide, width), 0) // length == iota((wide, width), 1) // HD, 1.0, 0.0
    )
    pair_lane = iota((1, 2 * HD), 1)
    left, right = ones_where(pair_lane < HD), ones_where(pair_lane >= HD)
    copies = ones_where(iota((2 * HD, width), 0) % HD == iota((2 * HD, width), 1) % HD)
    live = iota((span, wide), 0) < length + types

    def places(c):
        return (
            pl.ds(pl.multiple_of(c * length, length), length),
            pl.ds(pl.multiple_of(c * PAD, PAD), PAD),
            pl.ds(pl.multiple_of(c * span, PAD), span),
        )

    def diagonal(text):
        q = qs[text, :]
        return jnp.concatenate([q * lanes for lanes in head_lanes], axis=0)

    def forward_values(c):
        text, extra, both = places(c)
        q_diag = diagonal(text)
        k = jnp.concatenate([ks[text, :], kv[extra, :]], axis=0)
        v = jnp.concatenate([vs[text, :], vv[extra, :]], axis=0)
        g_rows = []
        for h in range(heads):
            block_g = g_ref[h, c]
            g_rows += [block_g * left, block_g * right]
        g_diag = (
            jnp.dot(jnp.concatenate(g_rows, axis=0), copies, preferred_element_type=F32) * own
        ).astype(BF16)
        scores = lax.dot_general(k, q_diag, ROWS_ROWS, preferred_element_type=F32) * scale
        scores = jnp.where(live, scores, -jnp.inf)
        grown = jnp.exp(scores - jnp.max(scores, axis=0, keepdims=True))
        probs = grown / jnp.sum(grown, axis=0, keepdims=True)
        low = probs.astype(BF16)
        prob_grads = lax.dot_general(v, g_diag, ROWS_ROWS, preferred_element_type=F32)
        dots = jnp.sum(prob_grads * probs, axis=0, keepdims=True)
        lows[both, :] = (probs * (prob_grads - dots) * scale).astype(BF16)
        dv_all = jnp.dot(low, g_diag, preferred_element_type=F32).astype(BF16)
        dv[text, :], dvv[extra, :] = dv_all[:length], dv_all[length:]
        out = (lax.dot_general(low, v, COLS_COLS, preferred_element_type=F32) * own).astype(BF16)
        flat = lax.dot_general(out, copies, ROWS_ROWS, preferred_element_type=F32)
        for h in range(heads):
            at = h * length
            ctx_ref[h, c] = jnp.where(
                pair_lane < HD, flat[at : at + half], flat[at + half : at + length]
            ).astype(BF16)

    def key_side(c):
        text, extra, both = places(c)
        dk_all = jnp.dot(lows[both, :], diagonal(text), preferred_element_type=F32).astype(BF16)
        dk[text, :], dkv[extra, :] = dk_all[:length], dk_all[length:]

    def query_side(c):
        text, extra, both = places(c)
        k = jnp.concatenate([ks[text, :], kv[extra, :]], axis=0)
        dq_all = lax.dot_general(lows[both, :], k, COLS_COLS, preferred_element_type=F32) * own
        dq_sum = dq_all[:length]
        for h in range(1, heads):
            dq_sum = dq_sum + dq_all[h * length : (h + 1) * length]
        dq[text, :] = dq_sum.astype(BF16)

    def over_centres(action, unroll):
        def several(i, carry):
            for j in range(unroll):
                action(i * unroll + j)
            return carry

        lax.fori_loop(0, centres // unroll, several, 0)

    def weight_part(grads, extra):
        part = lax.dot_general(grads[...], tok[...], COLS_COLS, preferred_element_type=F32)
        if extra is not None:
            part += lax.dot_general(extra[...], vpad[...], COLS_COLS, preferred_element_type=F32)
        return part

    over_centres(forward_values, UNROLL)
    part_ready(2, weight_part(dv, dvv))
    over_centres(key_side, 2 * UNROLL)
    part_ready(1, weight_part(dk, dkv))
    few_k = lax.dot_general(spread, dkv[...], COLS_COLS, preferred_element_type=F32).astype(BF16)
    few_v = lax.dot_general(spread, dvv[...], COLS_COLS, preferred_element_type=F32).astype(BF16)
    vg = jnp.dot(few_k, wk_ref[...], preferred_element_type=F32) + jnp.dot(
        few_v, wv_ref[...], preferred_element_type=F32
    )
    for i in range(m):
        vg_out[i] = vg[:, i * share : (i + 1) * share]

    def vg_copy(step):
        peer = lax.rem(my + step, m)
        return send(vg_out.at[peer], vg_in.at[my], vg_sems, (step,), "mp", peer)

    def sh_copy(step):
        held = shared.at[me]
        return send(held, held, sh_sems, (step,), "nodes", lax.rem(me + step, n))

    each(m, lambda step: vg_copy(step).start())
    vg_in[pl.ds(my, 1)] = vg_out[pl.ds(my, 1)]
    x_done(2)
    over_centres(query_side, 2 * UNROLL)
    part_ready(0, weight_part(dq, None))
    each(m, lambda step: vg_copy(step).wait())
    total = vg_in[0]
    for i in range(1, m):
        total = total + vg_in[i]
    shared[pl.ds(me, 1)] = (total / count_col).astype(BF16)[None]
    each(n, lambda step: sh_copy(step).start())
    x_done(1)
    z_done(2)
    x_done(0)
    z_done(1)
    a_done(2)
    z_done(0)
    a_done(1)
    each(n, lambda step: sh_copy(step).wait())
    shared_ref[...] = shared[...]
    a_done(0)
    for p in (2, 1, 0):
        f_done(p)
    weights_ref[...] = w_all[...]


def layer(n, m, types, tokens, w_query, w_key, w_value, grads, owned_cls, send_rows, slots, counts):
    heads, centres, half, _ = grads.shape
    count, model = tokens.shape
    width = heads * HD
    pairs, slot_width, rows = centres * types, slots.shape[2], owned_cls.shape[1]
    share = owned_cls.shape[0]
    vmem = pl.BlockSpec(memory_space=pltpu.VMEM)
    extra = centres * PAD
    zs = n // 2
    chunk = -(-(width * (model // LANES)) // (n * 16)) * 16
    narrow, small = pltpu.VMEM((count, width), BF16), pltpu.VMEM((extra, width), BF16)
    near = pltpu.VMEM((3, zs, chunk, LANES), BF16)
    all_parts = (3, 2, zs, chunk, LANES)
    dma = pltpu.SemaphoreType.DMA
    return pl.pallas_call(
        functools.partial(layer_kernel, n, m, types),
        out_shape=(
            jax.ShapeDtypeStruct(grads.shape, BF16),
            jax.ShapeDtypeStruct(all_parts, BF16),
            jax.ShapeDtypeStruct((n, pairs, share), BF16),
            jax.ShapeDtypeStruct((zs, rows, 2 * pairs), BF16),
        ),
        in_specs=[vmem] * 9,
        out_specs=(vmem,) * 4,
        scratch_shapes=[
            pltpu.VMEM((slot_width, pairs), F32),
            pltpu.VMEM((n, slot_width, pairs), F32),
            pltpu.VMEM((n, pairs, share), F32),
            pltpu.VMEM((n, pairs, share), F32),
            pltpu.VMEM((m, pairs, share), BF16),
            pltpu.VMEM((count, model), BF16), pltpu.VMEM((extra, model), BF16),
            narrow, narrow, narrow, small, small, narrow, narrow, narrow, small, small,
            pltpu.VMEM((count + extra, width), BF16),
            pltpu.VMEM(all_parts, BF16), near, near, near, pltpu.VMEM(all_parts, BF16),
            pltpu.VMEM((m, pairs, share), F32), pltpu.VMEM((m, pairs, share), F32),
            pltpu.VMEM((n, pairs, share), BF16),
            dma((2, n)), dma((2, n)), dma((2, m)), dma((2, m)), dma((2, n)),
            dma((2, 3)), dma((2, 3, zs)), dma((2, 3, zs)), dma((2, 3, zs)),
        ],
        compiler_params=pltpu.CompilerParams(
            collective_id=1, has_side_effects=True, vmem_limit_bytes=VMEM_LIMIT
        ),
        name="layer",
    )(tokens, w_query, w_key, w_value, grads, owned_cls, send_rows, slots, counts)


STEPS = 2


def finish_kernel(weights_ref, shared_ref, mix_ref, q_ref, k_ref, v_ref, cls_ref):
    width, model = q_ref.shape
    groups = mix_ref.shape[0]
    for p, out in enumerate((q_ref, k_ref, v_ref)):
        for i in range(model // LANES):
            out[:, i * LANES : (i + 1) * LANES] = weights_ref[
                p, i * width : (i + 1) * width, :
            ].astype(F32)

    def product(g):
        both = jnp.concatenate([shared_ref[2 * g], shared_ref[2 * g + 1]], axis=0)
        turned = both.astype(F32).T.astype(BF16)
        return lax.dot_general(turned, mix_ref[g], ROWS_ROWS, preferred_element_type=F32)

    cls_ref[...] = product(0)

    def group(g, carry):
        cls_ref[...] += product(g)
        return carry

    lax.fori_loop(1, groups, group, 0)


def finish(weights, shared, mix, width, model):
    weight = jax.ShapeDtypeStruct((width, model), F32)
    groups, rows, lanes = mix.shape
    share = shared.shape[2]
    part = width * model // LANES // STEPS
    weight_spec = pl.BlockSpec((width, model // STEPS), lambda i: (0, i))
    return pl.pallas_call(
        finish_kernel,
        grid=(STEPS,),
        out_shape=(weight, weight, weight, jax.ShapeDtypeStruct((share, rows), F32)),
        in_specs=[
            pl.BlockSpec((3, part, LANES), lambda i: (0, i, 0)),
            pl.BlockSpec(shared.shape, lambda i: (0, 0, 0)),
            pl.BlockSpec((groups, rows // STEPS, lanes), lambda i: (0, i, 0)),
        ],
        out_specs=(weight_spec, weight_spec, weight_spec,
                   pl.BlockSpec((share, rows // STEPS), lambda i: (0, i))),
        compiler_params=pltpu.CompilerParams(vmem_limit_bytes=VMEM_LIMIT),
        name="finish",
    )(weights, shared, mix)


def body(n, m, tokens, w_query, w_key, w_value, grad_out, owned_cls, send_rows, neigh_slot, neigh_count):
    centres, length, model = tokens.shape
    width = w_query.shape[0]
    heads = width // HD
    grads = grad_out.transpose(1, 0, 2).reshape(heads, centres, length // 2, 2 * HD)
    context, weights, shared, mix = layer(
        n, m, neigh_slot.shape[1], tokens.reshape(-1, model), w_query, w_key, w_value, grads,
        owned_cls, send_rows[0], neigh_slot, neigh_count.T,
    )
    grad_q, grad_k, grad_v, grad_cls = finish(
        weights.reshape(3, -1, LANES), shared, mix, width, model
    )
    context = context.reshape(heads, centres, length * HD).transpose(1, 0, 2)
    return context, grad_q, grad_k, grad_v, grad_cls


def solution(mesh):
    in_specs = (
        P("nodes", None, None),
        P("mp", None),
        P("mp", None),
        P("mp", None),
        P("nodes", "mp", None),
        P("mp", "nodes"),
        P("nodes", None, None),
        P("nodes", None, None),
        P("nodes", None),
    )
    out_specs = (
        P("nodes", "mp", None),
        P("mp", None),
        P("mp", None),
        P("mp", None),
        P("mp", "nodes"),
    )
    return jax.shard_map(
        functools.partial(body, mesh.shape["nodes"], mesh.shape["mp"]),
        mesh=mesh, in_specs=in_specs, out_specs=out_specs, check_vma=False,
    )
```

time: 128 us -> 101 us (0.79); the launches traced: 126 us -> 101 us
  Pallas kernels: 116 us -> 96 us
  local copies, waits for them, and re-layouts: 7.84 us -> 4.33 us
  other arithmetic: 1.54 us -> 0 us
    pallas_call x4 -> x2, Pallas kernels: 116 us -> 96 us  [the longest x1 90.8 us: layer(): pl.pallas_call(functools.partial(layer_kernel, n, m, types), out_shape=(j...]
    another operation x1 -> x0, local copies, waits for them, and re-layouts: 1.31 us -> none  [fetch(): send_rows.reshape(n // 2, 1, 2 * cap)]
    unnamed x2 -> x1, local copies, waits for them, and re-layouts: 2.93 us -> 2.17 us
where the time goes in v2:
time: 101 us
  Pallas kernels  96 us (95%)
  local copies, waits for them, and re-layouts  4.33 us (4%)
    pallas_call x1, Pallas kernels, layer(): pl.pallas_call(functools.partial(layer_kernel, n, m, types), out_shape=(j...  90.8 us
    pallas_call x1, Pallas kernels, finish(): pl.pallas_call(finish_kernel, grid=(STEPS,), out_shape=(weight, weight, w...  5.13 us
    unnamed x1, local copies, waits for them, and re-layouts  2.17 us
    reshape x1, local copies, waits for them, and re-layouts, body(): context = context.reshape(heads, centres, length * HD).transpose(1, 0, 2)  2.15 us

profile of v2, /device:TPU:0, one launch (start us, length us, event | category | flops | bytes accessed | tf_op | source)
XLA Modules:
  0.0 100.9 jit_solution(3811251700704392866)
XLA Ops:
  0.6 2.2 %copy.14 = bf16[12,8,32,128]{3,2,1,0:T(8,128)(2,1)} copy(bf16[12,8,32,128]{3,1,2,0:T(8,128)(2,1)} %bitcast.15) | data formatting | bytes 1572864
  2.8 90.8 %layer.1 = (bf16[3,32,32,128]{3,2,1,0:T(8,128)(2,1)}, bf16[3,2,4,144,128]{4,3,2,1,0:T(8,128)(2,1)}, bf16[8,64,192]{2,1,0:T(8,128)(2,1)}, bf16[4,2048,128]{2,1,0:T(8,128)(2,1)}) custom-call(bf16[2048,768]{1,0:T(8,128)(2,1)} %bitcast.13, bf16[192,768]{1,0:T(8,128)(2,1)} %wq_ref.1, bf16[192,768]{1,0:T(8,128)(2,1)} %wk_ref.1, bf16[192,768]{1,0:T(8,128)(2,1)} %wv_ref.1, ...), custom_call_target="tpu_custom_call" | custom-call | tf_op jit(solution)/shard_map/layer/pallas_call | solution.py:386
  93.7 2.2 %reshape.24 = bf16[3,32,4096]{2,1,0:T(8,128)(2,1)} reshape(bf16[3,32,32,128]{3,2,1,0:T(8,128)(2,1)} %get-tuple-element.13) | data formatting | bytes 1572864 | tf_op jit(solution)/shard_map/reshape | solution.py:478
  95.8 5.1 %finish.1 = (f32[192,768]{1,0:T(8,128)}, f32[192,768]{1,0:T(8,128)}, f32[192,768]{1,0:T(8,128)}, f32[192,2048]{1,0:T(8,128)}) custom-call(bf16[3,1152,128]{2,1,0:T(8,128)(2,1)} %bitcast.14, bf16[8,64,192]{2,1,0:T(8,128)(2,1)} %get-tuple-element.15.shared_ref, bf16[4,2048,128]{2,1,0:T(8,128)(2,1)} %get-tuple-element.16.mix_ref), custom_call_target="tpu_custom_call" | custom-call | tf_op jit(solution)/shard_map/finish/pallas_call | solution.py:450

commit v3 on v2

--- a/solution.py
+++ b/solution.py
@@ -63,7 +63,7 @@
     lax.fori_loop(1, size, one, 0)
 
 
-UNROLL = 2
+UNROLL = 4
 
 
 def layer_kernel(
@@ -71,7 +71,7 @@
     tok_ref, wq_ref, wk_ref, wv_ref, g_ref, cls_ref, send_ref, slot_ref, count_ref,
     ctx_ref, weights_ref, shared_ref, mix_ref,
     slots_own, slots, parts, arrived, cols,
-    tok, vpad, qs, ks, vs, kv, vv, dq, dk, dv, dkv, dvv, lows,
+    tok, vpad, qs, ks, vs, kv, vv, dq, dk, dv, dkv, dvv, lows, probs_all, g_all,
     wsum, x_in, z_sum, z_in, w_all, vg_out, vg_in, shared,
     slot_sems, part_sems, col_sems, vg_sems, sh_sems, x_sems, z_sems, a_sems, f_sems,
 ):
@@ -246,12 +246,13 @@
     scale = 1.0 / math.sqrt(HD)
     lane_head = iota((1, width), 1) // HD
     head_lanes = [ones_where(lane_head == h) for h in range(heads)]
-    own = jnp.where(
-        iota((wide, width), 0) // length == iota((wide, width), 1) // HD, 1.0, 0.0
-    )
+    own = ones_where(iota((wide, width), 0) // length == iota((wide, width), 1) // HD)
     pair_lane = iota((1, 2 * HD), 1)
     left, right = ones_where(pair_lane < HD), ones_where(pair_lane >= HD)
     copies = ones_where(iota((2 * HD, width), 0) % HD == iota((2 * HD, width), 1) % HD)
+    feature, flat_lane = iota((width, 2 * width), 0), iota((width, 2 * width), 1)
+    to_flat = (feature // HD) * 2 * HD + feature % HD
+    evens, odds = ones_where(flat_lane == to_flat), ones_where(flat_lane == to_flat + HD)
     live = iota((span, wide), 0) < length + types
 
     def places(c):
@@ -259,63 +260,87 @@
             pl.ds(pl.multiple_of(c * length, length), length),
             pl.ds(pl.multiple_of(c * PAD, PAD), PAD),
             pl.ds(pl.multiple_of(c * span, PAD), span),
+            pl.ds(pl.multiple_of(c * wide, length), wide),
         )
 
     def diagonal(text):
         q = qs[text, :]
         return jnp.concatenate([q * lanes for lanes in head_lanes], axis=0)
 
-    def forward_values(c):
-        text, extra, both = places(c)
-        q_diag = diagonal(text)
+    def compact(blocks):
+        picked = blocks[(heads - 1) * length :]
+        for h in range(heads - 2, -1, -1):
+            picked = jnp.where(lane_head == h, blocks[h * length : (h + 1) * length], picked)
+        return picked.astype(BF16)
+
+    def value_side(c):
+        text, extra, both, diag = places(c)
         k = jnp.concatenate([ks[text, :], kv[extra, :]], axis=0)
-        v = jnp.concatenate([vs[text, :], vv[extra, :]], axis=0)
         g_rows = []
         for h in range(heads):
             block_g = g_ref[h, c]
             g_rows += [block_g * left, block_g * right]
-        g_diag = (
-            jnp.dot(jnp.concatenate(g_rows, axis=0), copies, preferred_element_type=F32) * own
-        ).astype(BF16)
-        scores = lax.dot_general(k, q_diag, ROWS_ROWS, preferred_element_type=F32) * scale
+        g_diag = jnp.dot(
+            jnp.concatenate(g_rows, axis=0), copies, preferred_element_type=F32
+        ).astype(BF16) * own
+        g_all[diag, :] = g_diag
+        scores = lax.dot_general(k, diagonal(text), ROWS_ROWS, preferred_element_type=F32) * scale
         scores = jnp.where(live, scores, -jnp.inf)
         grown = jnp.exp(scores - jnp.max(scores, axis=0, keepdims=True))
-        probs = grown / jnp.sum(grown, axis=0, keepdims=True)
-        low = probs.astype(BF16)
-        prob_grads = lax.dot_general(v, g_diag, ROWS_ROWS, preferred_element_type=F32)
+        probs = grown * (1.0 / jnp.sum(grown, axis=0, keepdims=True))
+        probs_all[both, :] = probs
+        dv_all = jnp.dot(probs.astype(BF16), g_diag, preferred_element_type=F32).astype(BF16)
+        dv[text, :], dvv[extra, :] = dv_all[:length], dv_all[length:]
+
+    def key_side(c):
+        text, extra, both, diag = places(c)
+        v = jnp.concatenate([vs[text, :], vv[extra, :]], axis=0)
+        probs = probs_all[both, :]
+        prob_grads = lax.dot_general(v, g_all[diag, :], ROWS_ROWS, preferred_element_type=F32)
         dots = jnp.sum(prob_grads * probs, axis=0, keepdims=True)
-        lows[both, :] = (probs * (prob_grads - dots) * scale).astype(BF16)
-        dv_all = jnp.dot(low, g_diag, preferred_element_type=F32).astype(BF16)
-        dv[text, :], dvv[extra, :] = dv_all[:length], dv_all[length:]
-        out = (lax.dot_general(low, v, COLS_COLS, preferred_element_type=F32) * own).astype(BF16)
-        flat = lax.dot_general(out, copies, ROWS_ROWS, preferred_element_type=F32)
-        for h in range(heads):
-            at = h * length
-            ctx_ref[h, c] = jnp.where(
-                pair_lane < HD, flat[at : at + half], flat[at + half : at + length]
-            ).astype(BF16)
-
-    def key_side(c):
-        text, extra, both = places(c)
-        dk_all = jnp.dot(lows[both, :], diagonal(text), preferred_element_type=F32).astype(BF16)
+        low = (probs * (prob_grads - dots) * scale).astype(BF16)
+        lows[both, :] = low
+        dk_all = jnp.dot(low, diagonal(text), preferred_element_type=F32).astype(BF16)
         dk[text, :], dkv[extra, :] = dk_all[:length], dk_all[length:]
 
     def query_side(c):
-        text, extra, both = places(c)
+        text, extra, both, _ = places(c)
         k = jnp.concatenate([ks[text, :], kv[extra, :]], axis=0)
-        dq_all = lax.dot_general(lows[both, :], k, COLS_COLS, preferred_element_type=F32) * own
-        dq_sum = dq_all[:length]
-        for h in range(1, heads):
-            dq_sum = dq_sum + dq_all[h * length : (h + 1) * length]
-        dq[text, :] = dq_sum.astype(BF16)
-
-    def over_centres(action, unroll):
+        dq[text, :] = compact(
+            lax.dot_general(lows[both, :], k, COLS_COLS, preferred_element_type=F32)
+        )
+
+    def contexts(start, stop):
+        def some(i, carry):
+            even, odd = [], []
+            for j in range(UNROLL):
+                text, extra, both, _ = places(i * UNROLL + j)
+                v = jnp.concatenate([vs[text, :], vv[extra, :]], axis=0)
+                out = compact(lax.dot_general(
+                    probs_all[both, :].astype(BF16), v, COLS_COLS, preferred_element_type=F32
+                ))
+                even.append(out[:half])
+                odd.append(out[half:])
+            flat = jnp.dot(
+                jnp.concatenate(even, axis=0), evens, preferred_element_type=F32
+            ) + jnp.dot(jnp.concatenate(odd, axis=0), odds, preferred_element_type=F32)
+            flat = flat.astype(BF16)
+            for j in range(UNROLL):
+                for h in range(heads):
+                    ctx_ref[h, i * UNROLL + j] = flat[
+                        j * half : (j + 1) * half, h * 2 * HD : (h + 1) * 2 * HD
+                    ]
+            return carry
+
+        lax.fori_loop(start * centres // (4 * UNROLL), stop * centres // (4 * UNROLL), some, 0)
+
+    def over_centres(action, start, stop):
         def several(i, carry):
-            for j in range(unroll):
-                action(i * unroll + j)
+            for j in range(UNROLL):
+                action(i * UNROLL + j)
             return carry
 
-        lax.fori_loop(0, centres // unroll, several, 0)
+        lax.fori_loop(start * centres // (4 * UNROLL), stop * centres // (4 * UNROLL), several, 0)
 
     def weight_part(grads, extra):
         part = lax.dot_general(grads[...], tok[...], COLS_COLS, preferred_element_type=F32)
@@ -323,9 +348,11 @@
             part += lax.dot_general(extra[...], vpad[...], COLS_COLS, preferred_element_type=F32)
         return part
 
-    over_centres(forward_values, UNROLL)
+    over_centres(value_side, 0, 4)
     part_ready(2, weight_part(dv, dvv))
-    over_centres(key_side, 2 * UNROLL)
+    over_centres(key_side, 0, 2)
+    x_done(2)
+    over_centres(key_side, 2, 4)
     part_ready(1, weight_part(dk, dkv))
     few_k = lax.dot_general(spread, dkv[...], COLS_COLS, preferred_element_type=F32).astype(BF16)
     few_v = lax.dot_general(spread, dvv[...], COLS_COLS, preferred_element_type=F32).astype(BF16)
@@ -345,8 +372,8 @@
 
     each(m, lambda step: vg_copy(step).start())
     vg_in[pl.ds(my, 1)] = vg_out[pl.ds(my, 1)]
-    x_done(2)
-    over_centres(query_side, 2 * UNROLL)
+    over_centres(query_side, 0, 4)
+    z_done(2)
     part_ready(0, weight_part(dq, None))
     each(m, lambda step: vg_copy(step).wait())
     total = vg_in[0]
@@ -355,15 +382,18 @@
     shared[pl.ds(me, 1)] = (total / count_col).astype(BF16)[None]
     each(n, lambda step: sh_copy(step).start())
     x_done(1)
-    z_done(2)
+    contexts(0, 1)
     x_done(0)
+    a_done(2)
     z_done(1)
-    a_done(2)
+    contexts(1, 2)
     z_done(0)
     a_done(1)
+    contexts(2, 3)
     each(n, lambda step: sh_copy(step).wait())
     shared_ref[...] = shared[...]
     a_done(0)
+    contexts(3, 4)
     for p in (2, 1, 0):
         f_done(p)
     weights_ref[...] = w_all[...]
@@ -401,7 +431,8 @@
             pltpu.VMEM((m, pairs, share), BF16),
             pltpu.VMEM((count, model), BF16), pltpu.VMEM((extra, model), BF16),
             narrow, narrow, narrow, small, small, narrow, narrow, narrow, small, small,
-            pltpu.VMEM((count + extra, width), BF16),
+            pltpu.VMEM((count + extra, width), BF16), pltpu.VMEM((count + extra, width), F32),
+            pltpu.VMEM((count * heads, width), BF16),
             pltpu.VMEM(all_parts, BF16), near, near, near, pltpu.VMEM(all_parts, BF16),
             pltpu.VMEM((m, pairs, share), F32), pltpu.VMEM((m, pairs, share), F32),
             pltpu.VMEM((n, pairs, share), BF16),
@@ -409,7 +440,7 @@
             dma((2, 3)), dma((2, 3, zs)), dma((2, 3, zs)), dma((2, 3, zs)),
         ],
         compiler_params=pltpu.CompilerParams(
-            collective_id=1, has_side_effects=True, vmem_limit_bytes=VMEM_LIMIT
+            collective_id=1, has_side_effects=True, vmem_limit_bytes=VMEM_LIMIT + n // 16 * 3 * 2**19
         ),
         name="layer",
     )(tokens, w_query, w_key, w_value, grads, owned_cls, send_rows, slots, counts)

time: 101 us -> 98.2 us (0.972)
  Pallas kernels: 96 us -> 93 us
    pallas_call x1, Pallas kernels: 90.8 us -> 87.9 us  [layer(): pl.pallas_call(functools.partial(layer_kernel, n, m, types), out_shape=(j...]
where the time goes in v3:
time: 98.2 us; the launch traced here: 98 us
  Pallas kernels  93 us (95%)
  local copies, waits for them, and re-layouts  4.33 us (4%)
    pallas_call x1, Pallas kernels, layer(): pl.pallas_call(functools.partial(layer_kernel, n, m, types), out_shape=(j...  87.9 us
    pallas_call x1, Pallas kernels, finish(): pl.pallas_call(finish_kernel, grid=(STEPS,), out_shape=(weight, weight, w...  5.13 us
    unnamed x1, local copies, waits for them, and re-layouts  2.17 us
    reshape x1, local copies, waits for them, and re-layouts, body(): context = context.reshape(heads, centres, length * HD).transpose(1, 0, 2)  2.15 us

profile of v3, /device:TPU:0, one launch (start us, length us, event | category | flops | bytes accessed | tf_op | source)
XLA Modules:
  0.0 98.0 jit_solution(9101434285859250318)
XLA Ops:
  0.6 2.2 %copy.14 = bf16[12,8,32,128]{3,2,1,0:T(8,128)(2,1)} copy(bf16[12,8,32,128]{3,1,2,0:T(8,128)(2,1)} %bitcast.15) | data formatting | bytes 1572864
  2.8 87.9 %layer.1 = (bf16[3,32,32,128]{3,2,1,0:T(8,128)(2,1)}, bf16[3,2,4,144,128]{4,3,2,1,0:T(8,128)(2,1)}, bf16[8,64,192]{2,1,0:T(8,128)(2,1)}, bf16[4,2048,128]{2,1,0:T(8,128)(2,1)}) custom-call(bf16[2048,768]{1,0:T(8,128)(2,1)} %bitcast.13, bf16[192,768]{1,0:T(8,128)(2,1)} %wq_ref.1, bf16[192,768]{1,0:T(8,128)(2,1)} %wk_ref.1, bf16[192,768]{1,0:T(8,128)(2,1)} %wv_ref.1, ...), custom_call_target="tpu_custom_call" | custom-call | tf_op jit(solution)/shard_map/layer/pallas_call | solution.py:416
  90.7 2.2 %reshape.24 = bf16[3,32,4096]{2,1,0:T(8,128)(2,1)} reshape(bf16[3,32,32,128]{3,2,1,0:T(8,128)(2,1)} %get-tuple-element.13) | data formatting | bytes 1572864 | tf_op jit(solution)/shard_map/reshape | solution.py:509
  92.8 5.1 %finish.1 = (f32[192,768]{1,0:T(8,128)}, f32[192,768]{1,0:T(8,128)}, f32[192,768]{1,0:T(8,128)}, f32[192,2048]{1,0:T(8,128)}) custom-call(bf16[3,1152,128]{2,1,0:T(8,128)(2,1)} %bitcast.14, bf16[8,64,192]{2,1,0:T(8,128)(2,1)} %get-tuple-element.15.shared_ref, bf16[4,2048,128]{2,1,0:T(8,128)(2,1)} %get-tuple-element.16.mix_ref), custom_call_target="tpu_custom_call" | custom-call | tf_op jit(solution)/shard_map/finish/pallas_call | solution.py:481

commit v4 on v3

--- a/solution.py
+++ b/solution.py
@@ -71,7 +71,7 @@
     tok_ref, wq_ref, wk_ref, wv_ref, g_ref, cls_ref, send_ref, slot_ref, count_ref,
     ctx_ref, weights_ref, shared_ref, mix_ref,
     slots_own, slots, parts, arrived, cols,
-    tok, vpad, qs, ks, vs, kv, vv, dq, dk, dv, dkv, dvv, lows, probs_all, g_all,
+    tok, vpad, qs, ks, vs, kv, vv, dk, dv, dkv, dvv, probs_all, g_all,
     wsum, x_in, z_sum, z_in, w_all, vg_out, vg_in, shared,
     slot_sems, part_sems, col_sems, vg_sems, sh_sems, x_sems, z_sems, a_sems, f_sems,
 ):
@@ -189,59 +189,81 @@
         vpad[...], wv_ref[...], ROWS_ROWS, preferred_element_type=F32
     ).astype(BF16)
 
-    def x_copy(p):
-        return send(wsum.at[p, 1 - par], x_in.at[p], x_sems, (p,), "nodes", mate)
-
-    def z_copy(p, step):
+    units = model // LANES // 2
+    value_part, key_part = (0, 2 * units, units), (1, units, units)
+    query_parts = [(2 + i, i, 1) for i in range(units)]
+
+    def x_copy(part):
+        slot, at, size = part
+        some = pl.ds(at, size)
+        return send(wsum.at[1 - par, some], x_in.at[some], x_sems, (slot,), "nodes", mate)
+
+    def z_copy(part, step):
+        slot, at, size = part
+        some = pl.ds(at, size)
         peer = lax.rem(zz + step, zs)
-        return send(z_sum.at[p, peer], z_in.at[p, zz], z_sems, (p, step), "nodes", 2 * peer + par)
-
-    def a_copy(p, step):
-        own = w_all.at[p, par, zz]
-        return send(own, own, a_sems, (p, step), "nodes", 2 * lax.rem(zz + step, zs) + par)
-
-    def f_copy(p, step):
-        held = w_all.at[p, par, lax.rem(zz - step + zs, zs)]
-        return send(held, held, f_sems, (p, step), "nodes", mate)
-
-    def part_ready(p, part):
-        at = 0
-        flat = []
-        for lanes in range(0, model, LANES):
-            flat.append(part[:, lanes : lanes + LANES].astype(BF16))
-        flat = jnp.concatenate(flat, axis=0)
-        _, _, _, size, _ = wsum.shape
-        short = 2 * zs * size - flat.shape[0]
-        if short:
-            flat = jnp.concatenate([flat, jnp.zeros((short, LANES), BF16)], axis=0)
-        wsum[p] = flat.reshape(2, zs, size, LANES)
-        x_copy(p).start()
-
-    def x_done(p):
-        x_copy(p).wait()
-        z_sum[p] = (wsum[p, par].astype(F32) + x_in[p].astype(F32)).astype(BF16)
-        each(zs, lambda step: z_copy(p, step).start())
-        z_in[p, pl.ds(zz, 1)] = z_sum[p, pl.ds(zz, 1)]
-
-    def z_done(p):
-        each(zs, lambda step: z_copy(p, step).wait())
-        weights = z_in[p, 0].astype(F32)
+        return send(
+            z_sum.at[some, peer], z_in.at[some, zz], z_sems, (slot, step), "nodes", 2 * peer + par
+        )
+
+    def a_copy(part, step):
+        slot, at, size = part
+        held = w_all.at[par, pl.ds(at, size), zz]
+        return send(held, held, a_sems, (slot, step), "nodes", 2 * lax.rem(zz + step, zs) + par)
+
+    def f_copy(part, step):
+        slot, at, size = part
+        held = w_all.at[par, pl.ds(at, size), lax.rem(zz - step + zs, zs)]
+        return send(held, held, f_sems, (slot, step), "nodes", mate)
+
+    def ready(parts_of, at, grads, extra):
+        size = wsum.shape[2:]
+        for side in (1 - par, par):
+            lanes = pl.ds(pl.multiple_of(side * units * LANES, LANES), units * LANES)
+            part = lax.dot_general(
+                grads[...], tok[:, lanes], COLS_COLS, preferred_element_type=F32
+            )
+            if extra is not None:
+                part += lax.dot_general(
+                    extra[...], vpad[:, lanes], COLS_COLS, preferred_element_type=F32
+                )
+            for j in range(units):
+                flat = part[:, j * LANES : (j + 1) * LANES].astype(BF16)
+                short = size[0] * size[1] - width
+                if short:
+                    flat = jnp.concatenate([flat, jnp.zeros((short, LANES), BF16)], axis=0)
+                wsum[side, at + j] = flat.reshape(size)
+            if side is not par:
+                for one in parts_of:
+                    x_copy(one).start()
+
+    def x_done(part):
+        x_copy(part).wait()
+        some = pl.ds(part[1], part[2])
+        z_sum[some] = (wsum[par, some].astype(F32) + x_in[some].astype(F32)).astype(BF16)
+        each(zs, lambda step: z_copy(part, step).start())
+        z_in[some, pl.ds(zz, 1)] = z_sum[some, pl.ds(zz, 1)]
+
+    def z_done(part):
+        each(zs, lambda step: z_copy(part, step).wait())
+        some = pl.ds(part[1], part[2])
+        weights = z_in[some, 0].astype(F32)
         for b in range(1, zs):
-            weights = weights + z_in[p, b].astype(F32)
-        w_all[p, par, zz] = weights.astype(BF16)
-        each(zs, lambda step: a_copy(p, step).start())
-        f_copy(p, 0).start()
-
-    def a_done(p):
+            weights = weights + z_in[some, b].astype(F32)
+        w_all[par, some, zz] = weights.astype(BF16)
+        each(zs, lambda step: a_copy(part, step).start())
+        f_copy(part, 0).start()
+
+    def a_done(part):
         def forward(step):
-            a_copy(p, step).wait()
-            f_copy(p, step).start()
+            a_copy(part, step).wait()
+            f_copy(part, step).start()
 
         each(zs, forward)
 
-    def f_done(p):
-        f_copy(p, 0).wait()
-        each(zs, lambda step: f_copy(p, step).wait())
+    def f_done(part):
+        f_copy(part, 0).wait()
+        each(zs, lambda step: f_copy(part, step).wait())
 
     scale = 1.0 / math.sqrt(HD)
     lane_head = iota((1, width), 1) // HD
@@ -262,6 +284,9 @@
             pl.ds(pl.multiple_of(c * span, PAD), span),
             pl.ds(pl.multiple_of(c * wide, length), wide),
         )
+
+    def kept(c):
+        return pl.ds(pl.multiple_of(c * wide, length), span)
 
     def diagonal(text):
         q = qs[text, :]
@@ -299,15 +324,15 @@
         prob_grads = lax.dot_general(v, g_all[diag, :], ROWS_ROWS, preferred_element_type=F32)
         dots = jnp.sum(prob_grads * probs, axis=0, keepdims=True)
         low = (probs * (prob_grads - dots) * scale).astype(BF16)
-        lows[both, :] = low
+        g_all[kept(c), :] = low
         dk_all = jnp.dot(low, diagonal(text), preferred_element_type=F32).astype(BF16)
         dk[text, :], dkv[extra, :] = dk_all[:length], dk_all[length:]
 
     def query_side(c):
-        text, extra, both, _ = places(c)
+        text, extra, _, _ = places(c)
         k = jnp.concatenate([ks[text, :], kv[extra, :]], axis=0)
-        dq[text, :] = compact(
-            lax.dot_general(lows[both, :], k, COLS_COLS, preferred_element_type=F32)
+        qs[text, :] = compact(
+            lax.dot_general(g_all[kept(c), :], k, COLS_COLS, preferred_element_type=F32)
         )
 
     def contexts(start, stop):
@@ -342,18 +367,13 @@
 
         lax.fori_loop(start * centres // (4 * UNROLL), stop * centres // (4 * UNROLL), several, 0)
 
-    def weight_part(grads, extra):
-        part = lax.dot_general(grads[...], tok[...], COLS_COLS, preferred_element_type=F32)
-        if extra is not None:
-            part += lax.dot_general(extra[...], vpad[...], COLS_COLS, preferred_element_type=F32)
-        return part
-
     over_centres(value_side, 0, 4)
-    part_ready(2, weight_part(dv, dvv))
+    ready([value_part], 2 * units, dv, dvv)
     over_centres(key_side, 0, 2)
-    x_done(2)
+    x_done(value_part)
     over_centres(key_side, 2, 4)
-    part_ready(1, weight_part(dk, dkv))
+    z_done(value_part)
+    ready([key_part], units, dk, dkv)
     few_k = lax.dot_general(spread, dkv[...], COLS_COLS, preferred_element_type=F32).astype(BF16)
     few_v = lax.dot_general(spread, dvv[...], COLS_COLS, preferred_element_type=F32).astype(BF16)
     vg = jnp.dot(few_k, wk_ref[...], preferred_element_type=F32) + jnp.dot(
@@ -373,29 +393,31 @@
     each(m, lambda step: vg_copy(step).start())
     vg_in[pl.ds(my, 1)] = vg_out[pl.ds(my, 1)]
     over_centres(query_side, 0, 4)
-    z_done(2)
-    part_ready(0, weight_part(dq, None))
+    a_done(value_part)
+    x_done(key_part)
+    ready(query_parts, 0, qs, None)
     each(m, lambda step: vg_copy(step).wait())
     total = vg_in[0]
     for i in range(1, m):
         total = total + vg_in[i]
     shared[pl.ds(me, 1)] = (total / count_col).astype(BF16)[None]
     each(n, lambda step: sh_copy(step).start())
-    x_done(1)
+    z_done(key_part)
     contexts(0, 1)
-    x_done(0)
-    a_done(2)
-    z_done(1)
+    for part in query_parts:
+        x_done(part)
+    a_done(key_part)
     contexts(1, 2)
-    z_done(0)
-    a_done(1)
+    for part in query_parts:
+        z_done(part)
     contexts(2, 3)
+    for part in query_parts:
+        a_done(part)
     each(n, lambda step: sh_copy(step).wait())
     shared_ref[...] = shared[...]
-    a_done(0)
     contexts(3, 4)
-    for p in (2, 1, 0):
-        f_done(p)
+    for part in [value_part, key_part] + query_parts:
+        f_done(part)
     weights_ref[...] = w_all[...]
 
 
@@ -408,10 +430,12 @@
     vmem = pl.BlockSpec(memory_space=pltpu.VMEM)
     extra = centres * PAD
     zs = n // 2
-    chunk = -(-(width * (model // LANES)) // (n * 16)) * 16
+    chunk = -(-width // (zs * 16)) * 16
+    units = 3 * (model // LANES // 2)
+    slots_of = 2 + units // 3
     narrow, small = pltpu.VMEM((count, width), BF16), pltpu.VMEM((extra, width), BF16)
-    near = pltpu.VMEM((3, zs, chunk, LANES), BF16)
-    all_parts = (3, 2, zs, chunk, LANES)
+    near = pltpu.VMEM((units, zs, chunk, LANES), BF16)
+    all_parts = (2, units, zs, chunk, LANES)
     dma = pltpu.SemaphoreType.DMA
     return pl.pallas_call(
         functools.partial(layer_kernel, n, m, types),
@@ -430,17 +454,17 @@
             pltpu.VMEM((n, pairs, share), F32),
             pltpu.VMEM((m, pairs, share), BF16),
             pltpu.VMEM((count, model), BF16), pltpu.VMEM((extra, model), BF16),
-            narrow, narrow, narrow, small, small, narrow, narrow, narrow, small, small,
-            pltpu.VMEM((count + extra, width), BF16), pltpu.VMEM((count + extra, width), F32),
+            narrow, narrow, narrow, small, small, narrow, narrow, small, small,
+            pltpu.VMEM((count + extra, width), F32),
             pltpu.VMEM((count * heads, width), BF16),
             pltpu.VMEM(all_parts, BF16), near, near, near, pltpu.VMEM(all_parts, BF16),
             pltpu.VMEM((m, pairs, share), F32), pltpu.VMEM((m, pairs, share), F32),
             pltpu.VMEM((n, pairs, share), BF16),
             dma((2, n)), dma((2, n)), dma((2, m)), dma((2, m)), dma((2, n)),
-            dma((2, 3)), dma((2, 3, zs)), dma((2, 3, zs)), dma((2, 3, zs)),
+            dma((2, slots_of)), dma((2, slots_of, zs)), dma((2, slots_of, zs)), dma((2, slots_of, zs)),
         ],
         compiler_params=pltpu.CompilerParams(
-            collective_id=1, has_side_effects=True, vmem_limit_bytes=VMEM_LIMIT + n // 16 * 3 * 2**19
+            collective_id=1, has_side_effects=True, vmem_limit_bytes=VMEM_LIMIT + n // 16 * 7 * 2**18
         ),
         name="layer",
     )(tokens, w_query, w_key, w_value, grads, owned_cls, send_rows, slots, counts)
@@ -453,10 +477,9 @@
     width, model = q_ref.shape
     groups = mix_ref.shape[0]
     for p, out in enumerate((q_ref, k_ref, v_ref)):
-        for i in range(model // LANES):
-            out[:, i * LANES : (i + 1) * LANES] = weights_ref[
-                p, i * width : (i + 1) * width, :
-            ].astype(F32)
+        units = model // LANES
+        for i in range(units):
+            out[:, i * LANES : (i + 1) * LANES] = weights_ref[0, p * units + i].astype(F32)
 
     def product(g):
         both = jnp.concatenate([shared_ref[2 * g], shared_ref[2 * g + 1]], axis=0)
@@ -476,14 +499,13 @@
     weight = jax.ShapeDtypeStruct((width, model), F32)
     groups, rows, lanes = mix.shape
     share = shared.shape[2]
-    part = width * model // LANES // STEPS
     weight_spec = pl.BlockSpec((width, model // STEPS), lambda i: (0, i))
     return pl.pallas_call(
         finish_kernel,
         grid=(STEPS,),
         out_shape=(weight, weight, weight, jax.ShapeDtypeStruct((share, rows), F32)),
         in_specs=[
-            pl.BlockSpec((3, part, LANES), lambda i: (0, i, 0)),
+            pl.BlockSpec((1, weights.shape[1], width, LANES), lambda i: (i, 0, 0, 0)),
             pl.BlockSpec(shared.shape, lambda i: (0, 0, 0)),
             pl.BlockSpec((groups, rows // STEPS, lanes), lambda i: (0, i, 0)),
         ],
@@ -504,7 +526,7 @@
         owned_cls, send_rows[0], neigh_slot, neigh_count.T,
     )
     grad_q, grad_k, grad_v, grad_cls = finish(
-        weights.reshape(3, -1, LANES), shared, mix, width, model
+        weights.reshape(*weights.shape[:2], -1, LANES), shared, mix, width, model
     )
     context = context.reshape(heads, centres, length * HD).transpose(1, 0, 2)
     return context, grad_q, grad_k, grad_v, grad_cls

time: 98.2 us -> 97.8 us (level)
  no operation moved by 1% of the time
where the time goes in v4:
time: 97.8 us; the launch traced here: 97.6 us
  Pallas kernels  92.6 us (95%)
  local copies, waits for them, and re-layouts  4.33 us (4%)
    pallas_call x1, Pallas kernels, layer(): pl.pallas_call(functools.partial(layer_kernel, n, m, types), out_shape=(j...  87.5 us
    pallas_call x1, Pallas kernels, finish(): pl.pallas_call(finish_kernel, grid=(STEPS,), out_shape=(weight, weight, w...  5.13 us
    unnamed x1, local copies, waits for them, and re-layouts  2.17 us
    reshape x1, local copies, waits for them, and re-layouts, body(): context = context.reshape(heads, centres, length * HD).transpose(1, 0, 2)  2.15 us

profile of v4, /device:TPU:0, one launch (start us, length us, event | category | flops | bytes accessed | tf_op | source)
XLA Modules:
  0.0 97.6 jit_solution(12289820019200145913)
XLA Ops:
  0.6 2.2 %copy.14 = bf16[12,8,32,128]{3,2,1,0:T(8,128)(2,1)} copy(bf16[12,8,32,128]{3,1,2,0:T(8,128)(2,1)} %bitcast.15) | data formatting | bytes 1572864
  2.8 87.5 %layer.1 = (bf16[3,32,32,128]{3,2,1,0:T(8,128)(2,1)}, bf16[2,9,4,48,128]{4,3,2,1,0:T(8,128)(2,1)}, bf16[8,64,192]{2,1,0:T(8,128)(2,1)}, bf16[4,2048,128]{2,1,0:T(8,128)(2,1)}) custom-call(bf16[2048,768]{1,0:T(8,128)(2,1)} %bitcast.13, bf16[192,768]{1,0:T(8,128)(2,1)} %wq_ref.1, bf16[192,768]{1,0:T(8,128)(2,1)} %wk_ref.1, bf16[192,768]{1,0:T(8,128)(2,1)} %wv_ref.1, ...), custom_call_target="tpu_custom_call" | custom-call | tf_op jit(solution)/shard_map/layer/pallas_call | solution.py:440
  90.3 2.2 %reshape.24 = bf16[3,32,4096]{2,1,0:T(8,128)(2,1)} reshape(bf16[3,32,32,128]{3,2,1,0:T(8,128)(2,1)} %get-tuple-element.13) | data formatting | bytes 1572864 | tf_op jit(solution)/shard_map/reshape | solution.py:531
  92.5 5.1 %finish.1 = (f32[192,768]{1,0:T(8,128)}, f32[192,768]{1,0:T(8,128)}, f32[192,768]{1,0:T(8,128)}, f32[192,2048]{1,0:T(8,128)}) custom-call(bf16[2,9,192,128]{3,2,1,0:T(8,128)(2,1)} %bitcast.14, bf16[8,64,192]{2,1,0:T(8,128)(2,1)} %get-tuple-element.15.shared_ref, bf16[4,2048,128]{2,1,0:T(8,128)(2,1)} %get-tuple-element.16.mix_ref), custom_call_target="tpu_custom_call" | custom-call | tf_op jit(solution)/shard_map/finish/pallas_call | solution.py:503

commit v5 on v4

--- a/solution.py
+++ b/solution.py
@@ -134,7 +134,12 @@
     lane = iota((cap, 2 * pairs), 1)
     target = (iota((cap, 2 * pairs), 0) + me * cap).astype(F32)
 
-    def group(g, carry):
+    def part_copy(peer):
+        step = lax.rem(peer - me + n, n)
+        return send(parts.at[peer], arrived.at[me], part_sems, (step,), "nodes", peer)
+
+    def group(i, carry):
+        g = lax.rem(zz + 1 + i, zs)
         wanted = jnp.concatenate([slots[2 * g], slots[2 * g + 1]], axis=1)
         total = jnp.zeros((cap, 2 * pairs), F32)
         for k in range(slot_width):
@@ -151,23 +156,25 @@
                 hot, mixed, preferred_element_type=F32
             ).astype(BF16)
         turned = jnp.dot(cls_ref[...], mix_ref[g], preferred_element_type=F32).T
-        parts[2 * g] = turned[:pairs]
-        parts[2 * g + 1] = turned[pairs:]
+        turned = turned.astype(BF16)
+        for side in range(2):
+            peer = 2 * g + side
+            parts[peer] = turned[side * pairs : (side + 1) * pairs]
+
+            @pl.when(peer != me)
+            def _():
+                part_copy(peer).start()
+
         return carry
 
     lax.fori_loop(0, n // 2, group, 0)
 
-    def part_copy(step):
-        peer = lax.rem(me + step, n)
-        return send(parts.at[peer], arrived.at[me], part_sems, (step,), "nodes", peer)
-
-    each(n, lambda step: part_copy(step).start())
     arrived[pl.ds(me, 1)] = parts[pl.ds(me, 1)]
     lax.fori_loop(blocks // 2, blocks, project, 0)
-    each(n, lambda step: part_copy(step).wait())
-    total = arrived[0]
+    each(n, lambda step: part_copy(lax.rem(me + step, n)).wait())
+    total = arrived[0].astype(F32)
     for b in range(1, n):
-        total = total + arrived[b]
+        total = total + arrived[b].astype(F32)
     cols[pl.ds(my, 1)] = (total / count_col).astype(BF16)[None]
 
     def col_copy(step):
@@ -179,16 +186,6 @@
         ((spread_row % PAD) * centres + spread_row // PAD == iota((centres * PAD, pairs), 1))
         & (spread_row % PAD < types)
     )
-    each(m, lambda step: col_copy(step).wait())
-    virt = jnp.concatenate([cols[i].astype(F32) for i in range(m)], axis=1).astype(BF16)
-    vpad[...] = jnp.dot(spread, virt, preferred_element_type=F32).astype(BF16)
-    kv[...] = lax.dot_general(
-        vpad[...], wk_ref[...], ROWS_ROWS, preferred_element_type=F32
-    ).astype(BF16)
-    vv[...] = lax.dot_general(
-        vpad[...], wv_ref[...], ROWS_ROWS, preferred_element_type=F32
-    ).astype(BF16)
-
     units = model // LANES // 2
     value_part, key_part = (0, 2 * units, units), (1, units, units)
     query_parts = [(2 + i, i, 1) for i in range(units)]
@@ -298,9 +295,8 @@
             picked = jnp.where(lane_head == h, blocks[h * length : (h + 1) * length], picked)
         return picked.astype(BF16)
 
-    def value_side(c):
-        text, extra, both, diag = places(c)
-        k = jnp.concatenate([ks[text, :], kv[extra, :]], axis=0)
+    def lay_out(c):
+        _, _, _, diag = places(c)
         g_rows = []
         for h in range(heads):
             block_g = g_ref[h, c]
@@ -309,12 +305,16 @@
             jnp.concatenate(g_rows, axis=0), copies, preferred_element_type=F32
         ).astype(BF16) * own
         g_all[diag, :] = g_diag
+
+    def value_side(c):
+        text, extra, both, diag = places(c)
+        k = jnp.concatenate([ks[text, :], kv[extra, :]], axis=0)
         scores = lax.dot_general(k, diagonal(text), ROWS_ROWS, preferred_element_type=F32) * scale
         scores = jnp.where(live, scores, -jnp.inf)
         grown = jnp.exp(scores - jnp.max(scores, axis=0, keepdims=True))
         probs = grown * (1.0 / jnp.sum(grown, axis=0, keepdims=True))
         probs_all[both, :] = probs
-        dv_all = jnp.dot(probs.astype(BF16), g_diag, preferred_element_type=F32).astype(BF16)
+        dv_all = jnp.dot(probs.astype(BF16), g_all[diag, :], preferred_element_type=F32).astype(BF16)
         dv[text, :], dvv[extra, :] = dv_all[:length], dv_all[length:]
 
     def key_side(c):
@@ -367,6 +367,17 @@
 
         lax.fori_loop(start * centres // (4 * UNROLL), stop * centres // (4 * UNROLL), several, 0)
 
+    over_centres(lay_out, 0, 4)
+    each(m, lambda step: col_copy(step).wait())
+    virt = jnp.concatenate([cols[i].astype(F32) for i in range(m)], axis=1).astype(BF16)
+    vpad[...] = jnp.dot(spread, virt, preferred_element_type=F32).astype(BF16)
+    kv[...] = lax.dot_general(
+        vpad[...], wk_ref[...], ROWS_ROWS, preferred_element_type=F32
+    ).astype(BF16)
+    vv[...] = lax.dot_general(
+        vpad[...], wv_ref[...], ROWS_ROWS, preferred_element_type=F32
+    ).astype(BF16)
+
     over_centres(value_side, 0, 4)
     ready([value_part], 2 * units, dv, dvv)
     over_centres(key_side, 0, 2)
@@ -388,7 +399,16 @@
 
     def sh_copy(step):
         held = shared.at[me]
-        return send(held, held, sh_sems, (step,), "nodes", lax.rem(me + step, n))
+        peer = 2 * lax.rem(zz + step, zs) + par
+        return send(held, held, sh_sems, (0, step), "nodes", peer)
+
+    def sh_pass(step):
+        held = shared.at[2 * lax.rem(zz - step + zs, zs) + par]
+        return send(held, held, sh_sems, (1, step), "nodes", mate)
+
+    def sh_forward(step):
+        sh_copy(step).wait()
+        sh_pass(step).start()
 
     each(m, lambda step: vg_copy(step).start())
     vg_in[pl.ds(my, 1)] = vg_out[pl.ds(my, 1)]
@@ -401,21 +421,24 @@
     for i in range(1, m):
         total = total + vg_in[i]
     shared[pl.ds(me, 1)] = (total / count_col).astype(BF16)[None]
-    each(n, lambda step: sh_copy(step).start())
+    each(zs, lambda step: sh_copy(step).start())
+    sh_pass(0).start()
     z_done(key_part)
     contexts(0, 1)
     for part in query_parts:
         x_done(part)
     a_done(key_part)
+    each(zs, sh_forward)
     contexts(1, 2)
     for part in query_parts:
         z_done(part)
     contexts(2, 3)
     for part in query_parts:
         a_done(part)
-    each(n, lambda step: sh_copy(step).wait())
+    contexts(3, 4)
+    sh_pass(0).wait()
+    each(zs, lambda step: sh_pass(step).wait())
     shared_ref[...] = shared[...]
-    contexts(3, 4)
     for part in [value_part, key_part] + query_parts:
         f_done(part)
     weights_ref[...] = w_all[...]
@@ -450,8 +473,8 @@
         scratch_shapes=[
             pltpu.VMEM((slot_width, pairs), F32),
             pltpu.VMEM((n, slot_width, pairs), F32),
-            pltpu.VMEM((n, pairs, share), F32),
-            pltpu.VMEM((n, pairs, share), F32),
+            pltpu.VMEM((n, pairs, share), BF16),
+            pltpu.VMEM((n, pairs, share), BF16),
             pltpu.VMEM((m, pairs, share), BF16),
             pltpu.VMEM((count, model), BF16), pltpu.VMEM((extra, model), BF16),
             narrow, narrow, narrow, small, small, narrow, narrow, small, small,
@@ -460,7 +483,7 @@
             pltpu.VMEM(all_parts, BF16), near, near, near, pltpu.VMEM(all_parts, BF16),
             pltpu.VMEM((m, pairs, share), F32), pltpu.VMEM((m, pairs, share), F32),
             pltpu.VMEM((n, pairs, share), BF16),
-            dma((2, n)), dma((2, n)), dma((2, m)), dma((2, m)), dma((2, n)),
+            dma((2, n)), dma((2, n)), dma((2, m)), dma((2, m)), dma((2, 2, zs)),
             dma((2, slots_of)), dma((2, slots_of, zs)), dma((2, slots_of, zs)), dma((2, slots_of, zs)),
         ],
         compiler_params=pltpu.CompilerParams(

time: 97.8 us -> 85.8 us (0.88)
  Pallas kernels: 92.6 us -> 80.6 us
    pallas_call x1, Pallas kernels: 87.5 us -> 75.5 us  [layer(): pl.pallas_call(functools.partial(layer_kernel, n, m, types), out_shape=(j...]
where the time goes in v5:
time: 85.8 us; the launch traced here: 85.6 us
  Pallas kernels  80.6 us (94%)
  local copies, waits for them, and re-layouts  4.33 us (5%)
    pallas_call x1, Pallas kernels, layer(): pl.pallas_call(functools.partial(layer_kernel, n, m, types), out_shape=(j...  75.5 us
    pallas_call x1, Pallas kernels, finish(): pl.pallas_call(finish_kernel, grid=(STEPS,), out_shape=(weight, weight, w...  5.13 us
    unnamed x1, local copies, waits for them, and re-layouts  2.17 us
    reshape x1, local copies, waits for them, and re-layouts, body(): context = context.reshape(heads, centres, length * HD).transpose(1, 0, 2)  2.15 us

profile of v5, /device:TPU:0, one launch (start us, length us, event | category | flops | bytes accessed | tf_op | source)
XLA Modules:
  0.0 85.6 jit_solution(12841912838311642729)
XLA Ops:
  0.6 2.2 %copy.14 = bf16[12,8,32,128]{3,2,1,0:T(8,128)(2,1)} copy(bf16[12,8,32,128]{3,1,2,0:T(8,128)(2,1)} %bitcast.15) | data formatting | bytes 1572864
  2.8 75.5 %layer.1 = (bf16[3,32,32,128]{3,2,1,0:T(8,128)(2,1)}, bf16[2,9,4,48,128]{4,3,2,1,0:T(8,128)(2,1)}, bf16[8,64,192]{2,1,0:T(8,128)(2,1)}, bf16[4,2048,128]{2,1,0:T(8,128)(2,1)}) custom-call(bf16[2048,768]{1,0:T(8,128)(2,1)} %bitcast.13, bf16[192,768]{1,0:T(8,128)(2,1)} %wq_ref.1, bf16[192,768]{1,0:T(8,128)(2,1)} %wk_ref.1, bf16[192,768]{1,0:T(8,128)(2,1)} %wv_ref.1, ...), custom_call_target="tpu_custom_call" | custom-call | tf_op jit(solution)/shard_map/layer/pallas_call | solution.py:463
  78.3 2.2 %reshape.24 = bf16[3,32,4096]{2,1,0:T(8,128)(2,1)} reshape(bf16[3,32,32,128]{3,2,1,0:T(8,128)(2,1)} %get-tuple-element.13) | data formatting | bytes 1572864 | tf_op jit(solution)/shard_map/reshape | solution.py:554
  80.5 5.1 %finish.1 = (f32[192,768]{1,0:T(8,128)}, f32[192,768]{1,0:T(8,128)}, f32[192,768]{1,0:T(8,128)}, f32[192,2048]{1,0:T(8,128)}) custom-call(bf16[2,9,192,128]{3,2,1,0:T(8,128)(2,1)} %bitcast.14, bf16[8,64,192]{2,1,0:T(8,128)(2,1)} %get-tuple-element.15.shared_ref, bf16[4,2048,128]{2,1,0:T(8,128)(2,1)} %get-tuple-element.16.mix_ref), custom_call_target="tpu_custom_call" | custom-call | tf_op jit(solution)/shard_map/finish/pallas_call | solution.py:526
